TPU v7x, 256 devices: a whole 4x4x8 slice. The times are simulated.
256 devices in a mesh: seq: 32 (over z, y), ch: 8 (over x, core).
Axes of the slice: x: 4, y: 4, z: 8, core: 2. Of those that a mesh axis runs over, the one named last changes fastest.
Arguments:
- signal: float32 [32768, 1536], P('seq', 'ch'), may hold values from -6 to 6
- cotangent: float32 [32768, 1536], P('seq', 'ch'), may hold values from -6 to 6
- kernel_q: float32 [3, 1536], P(None, 'ch'), may hold values from -3 to 3
- kernel_k: float32 [3, 1536], P(None, 'ch'), may hold values from -3 to 3
- block_first: float32 [32, 1024, 1024], P('seq'), may hold values from -0.1875 to 0.1875
- block_second: float32 [32, 1024, 1024], P('seq'), may hold values from -0.1875 to 0.1875
- mix_self: float32 [5, 32, 1536], P(None, 'seq', 'ch'), may hold values from 0.5 to 1
- mix_partner: float32 [5, 32, 1536], P(None, 'seq', 'ch'), may hold values from -1 to 1
Outputs:
- output: float32 [32768, 1536], P('seq', 'ch')
- grad_signal: float32 [32768, 1536], P('seq', 'ch')
- grad_kernel_q: float32 [3, 1536], P(None, 'ch')
- grad_kernel_k: float32 [3, 1536], P(None, 'ch')
- grad_block_first: float32 [32, 1024, 1024], P('seq', 'ch')
- grad_block_second: float32 [32, 1024, 1024], P('seq', 'ch')
- grad_mix_self: float32 [5, 32, 1536], P(None, 'seq', 'ch')
- grad_mix_partner: float32 [5, 32, 1536], P(None, 'seq', 'ch')
All inputs are finite; a program needn't handle non-finite values.
Results may differ from a plain program's by a relative error of at most 0.00015.
Values sent between devices are 32-bit elements; how exact they have to be, the bound alone decides.
No kernel may reach another device: no remote copies, remote signals or barrier semaphores. Data moves between devices by JAX's collectives and lax.ppermute only.
A program may use at most 128 MiB of HBM per device.

v0:
```python
import math

import jax
import jax.numpy as jnp
from jax import lax
from jax.experimental import pallas as pl
from jax.experimental.pallas import tpu as pltpu
from jax.sharding import PartitionSpec as P

D = 1536
SECTIONS = 5
BLOCKS = 32
PARTS = ((0, 4), (4, 6))
LANE_OF_PART = (0, 64)
WEIGHT_TILE = 6
CHIPS = 4
STEPS = (2, 1, 3, 0)
COLUMNS = 256
VMEM_LIMIT = 56 * 1024 * 1024
WIDTH_SCALE = 1.0 / math.sqrt(D)
ROW_SCALE = 1.0 / math.sqrt(1024)
TOKEN_SCALE = 1.0 / math.sqrt(32768)

def flip(values, section):
    stride = 2**section
    pieces = []
    for at in range(0, BLOCKS, 2 * stride):
        pieces.append(values[at + stride : at + 2 * stride])
        pieces.append(values[at : at + stride])
    return jnp.concatenate(pieces, axis=0)


def load_weights(in_ref, weight_ref):
    for part in range(2):
        for at in range(2 * SECTIONS):
            lane = LANE_OF_PART[part] + at
            column = in_ref[:, 12, :, lane : lane + 1]
            weight_ref[part, at] = jnp.broadcast_to(column, (BLOCKS, 8, 128))


def step_forward(level, weight_ref, part, section):
    return (
        weight_ref[part, section] * level
        + weight_ref[part, SECTIONS + section] * flip(level, section)
    )


def forward_kernel(in_ref, out_ref, weight_ref):
    load_weights(in_ref, weight_ref)
    for part, (low, high) in enumerate(PARTS):

        def one_tile(tile, carry):
            level = in_ref[:, tile]
            for section in range(SECTIONS):
                level = step_forward(level, weight_ref, part, section)
            out_ref[:, tile] = level
            return carry

        lax.fori_loop(low, high, one_tile, 0)


def backward_kernel(in_ref, out_ref, weight_ref, level_ref, sum_ref):
    load_weights(in_ref, weight_ref)
    for part, (low, high) in enumerate(PARTS):

        def one_tile(tile, first):
            level = in_ref[:, tile]
            for section in range(SECTIONS):
                level_ref[section] = level
                if section < SECTIONS - 1:
                    level = step_forward(level, weight_ref, part, section)
            grad = in_ref[:, 6 + tile]
            for section in reversed(range(SECTIONS)):
                level = level_ref[section]
                own = grad * level
                other = grad * flip(level, section)
                if first:
                    sum_ref[part, section] = own
                    sum_ref[part, SECTIONS + section] = other
                else:
                    sum_ref[part, section] += own
                    sum_ref[part, SECTIONS + section] += other
                grad = weight_ref[part, section] * grad + flip(
                    weight_ref[part, SECTIONS + section] * grad, section
                )
            out_ref[:, tile] = grad

        one_tile(low, True)

        def body(tile, carry):
            one_tile(tile, False)
            return carry

        lax.fori_loop(low + 1, high, body, 0)

    lanes = lax.broadcasted_iota(jnp.int32, (BLOCKS, 8, 128), 2)
    result = jnp.zeros((BLOCKS, 8, 128), jnp.float32)
    for part in range(2):
        for at in range(2 * SECTIONS):
            total = jnp.sum(sum_ref[part, at], axis=2, keepdims=True)
            result = jnp.where(lanes == LANE_OF_PART[part] + at, total, result)
    out_ref[:, WEIGHT_TILE] = result


WEIGHT_SCRATCH = (2, 2 * SECTIONS, BLOCKS, 8, 128)
IN_VMEM = pl.BlockSpec(memory_space=pltpu.VMEM)


def butterfly_forward(tiles):
    return pl.pallas_call(
        forward_kernel,
        out_shape=jax.ShapeDtypeStruct((BLOCKS, 6, 8, 128), jnp.float32),
        in_specs=[IN_VMEM],
        out_specs=IN_VMEM,
        scratch_shapes=[pltpu.VMEM(WEIGHT_SCRATCH, jnp.float32)],
        compiler_params=pltpu.CompilerParams(vmem_limit_bytes=24 * 1024 * 1024),
        cost_estimate=pl.CostEstimate(flops=4_000_000, bytes_accessed=1_800_000, transcendentals=0),
        name="butterfly_forward",
    )(tiles)


def butterfly_backward(tiles):
    return pl.pallas_call(
        backward_kernel,
        out_shape=jax.ShapeDtypeStruct((BLOCKS, 7, 8, 128), jnp.float32),
        in_specs=[IN_VMEM],
        out_specs=IN_VMEM,
        scratch_shapes=[
            pltpu.VMEM(WEIGHT_SCRATCH, jnp.float32),
            pltpu.VMEM((SECTIONS, BLOCKS, 8, 128), jnp.float32),
            pltpu.VMEM(WEIGHT_SCRATCH, jnp.float32),
        ],
        compiler_params=pltpu.CompilerParams(vmem_limit_bytes=32 * 1024 * 1024),
        cost_estimate=pl.CostEstimate(flops=12_000_000, bytes_accessed=2_600_000, transcendentals=0),
        name="butterfly_backward",
    )(tiles)


def neighbours(low, high):
    count = lax.axis_size("seq")
    before = lax.ppermute(low, "seq", [(i, i + 1) for i in range(count - 1)])
    after = lax.ppermute(high, "seq", [(i + 1, i) for i in range(count - 1)])
    return before, after


def owner_and_tile(group, chunk):
    if group < 16:
        return 2 * group + chunk // 4, chunk % 4
    return 4 * (group - 16) + chunk // 2, 4 + chunk % 2


def split_two(values):
    high = values.astype(jnp.bfloat16)
    return high, (values - high.astype(jnp.float32)).astype(jnp.bfloat16)


def dot_three(left, right, left_dim, right_dim):
    def dot(a, b):
        return lax.dot_general(
            a, b, (((left_dim,), (right_dim,)), ((), ())), preferred_element_type=jnp.float32
        )

    (left_high, left_low), (right_high, right_low) = left, right
    return dot(left_high, right_high) + (dot(left_high, right_low) + dot(left_low, right_high))


def unpack(tile_ref, dest_ref, row):
    for group in range(24):
        for chunk in range(8):
            owner, tile = owner_and_tile(group, chunk)
            dest_ref[row + 8 * group : row + 8 * group + 8, 128 * chunk : 128 * chunk + 128] = (
                tile_ref[owner, tile]
            )


def chunk_of_step(place_ref, step):
    place = place_ref[0]
    return 2 * ((place // 2 + step) % CHIPS) + place % 2


def second_kernel(place_ref, left_a, left_b, right_a, right_b, *refs):
    outs, (right_ref,) = refs[:CHIPS], refs[CHIPS:]
    unpack(right_a, right_ref, 0)
    unpack(right_b, right_ref, 192)
    right = split_two(right_ref[...])
    for step in STEPS:
        rows = pl.ds(pl.multiple_of(chunk_of_step(place_ref, step) * 128, 128), 128)
        left = jnp.concatenate([left_a[:, rows], left_b[:, rows]], axis=0) * WIDTH_SCALE
        outs[step][...] = dot_three(split_two(left), right, 0, 0)


def first_kernel(place_ref, tiles_a, tiles_b, right_a, right_b, *refs):
    outs, (left_ref, tile_ref, right_ref, sem) = refs[:CHIPS], refs[CHIPS:]
    copies = []
    for half, (tiles, right) in enumerate(((tiles_a, right_a), (tiles_b, right_b))):
        copies.append(pltpu.make_async_copy(right, right_ref.at[half], sem.at[2 * half]))
        copies.append(pltpu.make_async_copy(tiles, tile_ref.at[half], sem.at[2 * half + 1]))
    for copy in copies:
        copy.start()
    for half in range(2):
        copies[2 * half].wait()
        right = split_two(right_ref[half])
        copies[2 * half + 1].wait()
        for step in STEPS:
            chunk = chunk_of_step(place_ref, step)
            for group in range(24):
                owner, tile = owner_and_tile(group, chunk)
                left_ref[step, 8 * group : 8 * group + 8, :] = tile_ref[half, owner, tile]
            product = dot_three(split_two(left_ref[step] * WIDTH_SCALE), right, 0, 0)
            if half == 0:
                outs[step][...] = product
            else:
                outs[step][...] += product


def first_products(place, tiles, tiles_other, gated, gated_other):
    piece = jax.ShapeDtypeStruct((128, 1024), jnp.float32)
    return pl.pallas_call(
        first_kernel,
        out_shape=[piece] * CHIPS,
        in_specs=[pl.BlockSpec(memory_space=pltpu.SMEM)] + [IN_HBM] * 4,
        out_specs=[pl.BlockSpec()] * CHIPS,
        scratch_shapes=[
            pltpu.VMEM((CHIPS, 192, 128), jnp.float32),
            pltpu.VMEM((2,) + tiles.shape, jnp.float32),
            pltpu.VMEM((2,) + gated.shape, jnp.float32),
            pltpu.SemaphoreType.DMA((4,)),
        ],
        compiler_params=pltpu.CompilerParams(vmem_limit_bytes=VMEM_LIMIT),
        cost_estimate=pl.CostEstimate(flops=1_200_000_000, bytes_accessed=5_000_000, transcendentals=0),
        name="block_first_products",
    )(place, tiles, tiles_other, gated, gated_other)


def shifted(values, before, after):
    width = values.shape[1]
    lanes = lax.broadcasted_iota(jnp.int32, values.shape, 1)
    prev = jnp.where(lanes == 0, before, pltpu.roll(values, 1, 1))
    return prev, jnp.where(lanes == width - 1, after, pltpu.roll(values, width - 1, 1))


def conv(column_ref, tap, prev, values, later):
    return (
        column_ref[:, tap : tap + 1] * prev
        + column_ref[:, tap + 1 : tap + 2] * values
        + column_ref[:, tap + 2 : tap + 3] * later
    )


def strips(ref, buffer, sem, first, along):
    copies = []
    for at in range(4):
        part = pl.ds(256 * at, 256)
        index = (part, slice(None)) if along == 0 else (slice(None), part)
        copies.append(pltpu.make_async_copy(ref.at[index], buffer.at[index], sem.at[first + at]))
    return copies


IN_HBM = pl.BlockSpec(memory_space=pl.ANY)


def prologue_kernel(
    signal_ref, cot_ref, before_ref, after_ref, taps_q_ref, taps_k_ref, self_ref, partner_ref, first_ref, second_ref,
    packed_ref, gated_ref, mixed_ref, halo_ref, column_ref,
    gated_high, gated_low, mixed_high, mixed_low,
):
    at = pl.program_id(0)

    @pl.when(at == 0)
    def _():
        values = signal_ref[...]
        rows = [taps_q_ref[...], taps_k_ref[...]]
        rows += [ref[section] for ref in (self_ref, partner_ref) for section in range(SECTIONS)]
        rows.append(jnp.zeros((112, values.shape[0]), jnp.float32))
        column_ref[...] = jnp.concatenate(rows, axis=0).T
        before = jnp.broadcast_to(before_ref[...], (128, values.shape[0])).T
        after = jnp.broadcast_to(after_ref[...], (128, values.shape[0])).T
        narrow = lax.broadcasted_iota(jnp.int32, before.shape, 1)
        halo_ref[...] = jnp.where(narrow == 0, before, after)
        prev, later = shifted(values, before[:, :1], after[:, :1])
        gated = conv(column_ref, 3, prev, values, later) * values
        gated_ref[...] = gated
        gated_high[...], gated_low[...] = split_two(gated)
        mixed = cot_ref[...] * conv(column_ref, 0, prev, values, later)
        mixed_ref[...] = mixed
        mixed_high[...], mixed_low[...] = split_two(mixed)
        weights = jnp.concatenate(
            [column_ref[:, 6:16], jnp.zeros((values.shape[0], 118), jnp.float32)], axis=1
        )
        moved = pltpu.roll(weights[128:192], 64, 1)
        for owner in range(BLOCKS):
            low, high = 8 * (owner // 2), 8 * (owner // 4)
            packed_ref[owner, 12] = weights[low : low + 8] + moved[high : high + 8]

    level = dot_three((gated_high[...], gated_low[...]), split_two(first_ref[0]), 1, 1)
    grad = dot_three((mixed_high[...], mixed_low[...]), split_two(second_ref[0]), 1, 0)
    for part in range(COLUMNS // 128):
        chunk = at * (COLUMNS // 128) + part
        for group in range(24):
            owner, tile = owner_and_tile(group, chunk)
            rows, lanes = slice(8 * group, 8 * group + 8), slice(128 * part, 128 * part + 128)
            packed_ref[owner, tile] = level[rows, lanes]
            packed_ref[owner, 6 + tile] = grad[rows, lanes]


def prologue(signal, cotangent, before, after, taps_q, taps_k, mix_self, mix_partner, first, second):
    breadth, height = signal.shape
    whole = lambda shape: pl.BlockSpec(shape, lambda i: (0,) * len(shape))
    full = jax.ShapeDtypeStruct(signal.shape, jnp.float32)
    packed = (BLOCKS, 13, 8, 128)
    return pl.pallas_call(
        prologue_kernel,
        grid=(height // COLUMNS,),
        out_shape=[jax.ShapeDtypeStruct(packed, jnp.float32)]
        + [full] * 2
        + [jax.ShapeDtypeStruct((breadth, 128), jnp.float32)] * 2,
        in_specs=[
            whole(signal.shape),
            whole(signal.shape),
            whole(before.shape),
            whole(after.shape),
            whole(taps_q.shape),
            whole(taps_k.shape),
            whole(mix_self.shape),
            whole(mix_partner.shape),
            pl.BlockSpec((1, COLUMNS, height), lambda i: (0, i, 0)),
            pl.BlockSpec((1, height, COLUMNS), lambda i: (0, 0, i)),
        ],
        out_specs=[whole(packed)] + [whole(signal.shape)] * 2 + [whole((breadth, 128))] * 2,
        scratch_shapes=[pltpu.VMEM(signal.shape, jnp.bfloat16)] * 4,
        compiler_params=pltpu.CompilerParams(vmem_limit_bytes=VMEM_LIMIT),
        cost_estimate=pl.CostEstimate(flops=2_400_000_000, bytes_accessed=15_000_000, transcendentals=0),
        name="prologue",
    )(signal, cotangent, before, after, taps_q, taps_k, mix_self, mix_partner, first, second)


def block_products(kernel, scratch, name, place, *operands):
    piece = jax.ShapeDtypeStruct((128, 1024), jnp.float32)
    return pl.pallas_call(
        kernel,
        out_shape=[piece] * CHIPS,
        in_specs=[pl.BlockSpec(memory_space=pltpu.SMEM)] + [pl.BlockSpec()] * 4,
        out_specs=[pl.BlockSpec()] * CHIPS,
        scratch_shapes=[pltpu.VMEM(scratch, jnp.float32)],
        compiler_params=pltpu.CompilerParams(vmem_limit_bytes=VMEM_LIMIT),
        cost_estimate=pl.CostEstimate(flops=1_200_000_000, bytes_accessed=5_000_000, transcendentals=0),
        name=name,
    )(place, *operands)


def other_core(values):
    return lax.ppermute(values, "ch", [(i, i ^ 1) for i in range(2 * CHIPS)])


def receive_pieces(pieces):
    return [
        lax.ppermute(pieces[step], "ch", [(i, (i + 2 * step) % (2 * CHIPS)) for i in range(2 * CHIPS)])
        for step in STEPS[:-1]
    ]


def tap_products(values, prev, here, later):
    out = []
    for other in (prev, here, later):
        product = values * other
        total = product[:, :128]
        for at in range(128, product.shape[1], 128):
            total = total + product[:, at : at + 128]
        out.append(total)
    return out


def small_columns(sums, first, last, lane):
    lanes = lax.broadcasted_iota(jnp.int32, sums[0].shape, 1)
    total = jnp.zeros(sums[0].shape, jnp.float32)
    for j, value in enumerate(sums):
        total = jnp.where(lanes == lane + j, jnp.sum(value, axis=1, keepdims=True), total)
    total = jnp.where(lanes == lane + 3, first, total)
    return jnp.where(lanes == lane + 4, last, total)


def output_kernel(
    column_ref, halo_ref, tile_hbm, block_hbm, signal_hbm, cot_hbm,
    out_hbm, grad_hbm, small_ref,
    tile_ref, block_ref, signal_ref, cot_ref, level_ref, out_ref, grad_ref, sem,
):
    get_tiles = pltpu.make_async_copy(tile_hbm, tile_ref, sem.at[0])
    get_signal = pltpu.make_async_copy(signal_hbm, signal_ref, sem.at[1])
    get_cot = pltpu.make_async_copy(cot_hbm, cot_ref, sem.at[2])
    get_block = strips(block_hbm.at[0], block_ref, sem, 3, 0)
    get_tiles.start()
    get_signal.start()
    get_block[0].start()
    get_cot.start()
    for copy in get_block[1:]:
        copy.start()
    get_tiles.wait()
    unpack(tile_ref, level_ref, 0)
    left = split_two(level_ref[...])
    get_signal.wait()
    values = signal_ref[...]
    prev, later = shifted(values, halo_ref[:, 0:1], halo_ref[:, 1:2])
    query = conv(column_ref, 0, prev, values, later)
    sums, puts = None, []
    for at in range(4):
        part = slice(256 * at, 256 * at + 256)
        get_block[at].wait()
        mixed = dot_three(left, split_two(block_ref[part, :]), 1, 1)
        if at == 0:
            get_cot.wait()
        out_ref[:, part] = query[:, part] * mixed
        grad = cot_ref[:, part] * mixed
        grad_ref[:, part] = grad
        for index, (ref, hbm) in enumerate(((out_ref, out_hbm), (grad_ref, grad_hbm))):
            put = pltpu.make_async_copy(ref.at[:, part], hbm.at[:, part], sem.at[7 + 2 * at + index])
            put.start()
            puts.append(put)
        new = tap_products(grad, prev[:, part], values[:, part], later[:, part])
        sums = new if sums is None else [a + b for a, b in zip(sums, new)]
    small_ref[...] = small_columns(sums, grad_ref[:, 0:1], grad_ref[:, 1023:1024], 0)
    for put in puts:
        put.wait()


def make_output(tiles, block, cotangent, signal, columns, halo):
    full = jax.ShapeDtypeStruct(signal.shape, jnp.float32)
    buffer = pltpu.VMEM(signal.shape, jnp.float32)
    return pl.pallas_call(
        output_kernel,
        out_shape=[full, full, jax.ShapeDtypeStruct((signal.shape[0], 128), jnp.float32)],
        in_specs=[pl.BlockSpec()] * 2 + [IN_HBM] * 4,
        out_specs=[IN_HBM] * 2 + [pl.BlockSpec()],
        scratch_shapes=[
            pltpu.VMEM(tiles.shape, jnp.float32),
            pltpu.VMEM(block.shape[1:], jnp.float32),
            buffer,
            buffer,
            buffer,
            buffer,
            buffer,
            pltpu.SemaphoreType.DMA((15,)),
        ],
        compiler_params=pltpu.CompilerParams(vmem_limit_bytes=VMEM_LIMIT),
        cost_estimate=pl.CostEstimate(flops=1_200_000_000, bytes_accessed=9_000_000, transcendentals=0),
        name="make_output",
    )(columns, halo, tiles, block, signal, cotangent)


def tap_kernel(halo_ref, signal_ref, block_ref, out_ref, ends_ref, edge_ref, high_ref, low_ref):
    at = pl.program_id(0)
    breadth = signal_ref.shape[0]

    @pl.when(at == 0)
    def _():
        values = signal_ref[...]
        prev, later = shifted(values, halo_ref[:, 0:1], halo_ref[:, 1:2])
        for j, other in enumerate((prev, values, later)):
            rows = slice(breadth * j, breadth * j + breadth)
            high_ref[rows, :], low_ref[rows, :] = split_two(values * other)
        lanes = lax.broadcasted_iota(jnp.int32, (breadth, 128), 1)
        ends_ref[...] = jnp.where(lanes == 0, values[:, :1], values[:, 1023:1024])

    block = block_ref[0]
    out_ref[...] = dot_three((high_ref[...], low_ref[...]), split_two(block), 1, 1)
    first = block[:, 0:128].T
    last = block[:, 896:1024].T
    edge_ref[0:8, :] = jnp.broadcast_to(first[0:1], (8, first.shape[1]))
    edge_ref[8:16, :] = jnp.broadcast_to(last[127:128], (8, first.shape[1]))


def tap_weights(signal, halo, block):
    breadth, height = signal.shape
    whole = lambda shape: pl.BlockSpec(shape, lambda i: (0,) * len(shape))
    return pl.pallas_call(
        tap_kernel,
        grid=(height // COLUMNS,),
        out_shape=[
            jax.ShapeDtypeStruct((3 * breadth, height), jnp.float32),
            jax.ShapeDtypeStruct((breadth, 128), jnp.float32),
            jax.ShapeDtypeStruct((16, height), jnp.float32),
        ],
        in_specs=[
            whole(halo.shape),
            whole(signal.shape),
            pl.BlockSpec((1, COLUMNS, height), lambda i: (0, i, 0)),
        ],
        out_specs=[
            pl.BlockSpec((3 * breadth, COLUMNS), lambda i: (0, i)),
            whole((breadth, 128)),
            pl.BlockSpec((16, COLUMNS), lambda i: (0, i)),
        ],
        scratch_shapes=[pltpu.VMEM((3 * breadth, height), jnp.bfloat16)] * 2,
        compiler_params=pltpu.CompilerParams(vmem_limit_bytes=VMEM_LIMIT),
        cost_estimate=pl.CostEstimate(flops=3_600_000_000, bytes_accessed=8_000_000, transcendentals=0),
        name="tap_weights",
    )(halo, signal, block)


def send_kernel(tile_ref, weight_ref, ends_ref, edge_ref, small_in_ref, send_ref):
    breadth = ends_ref.shape[0]
    totals = [[] for _ in range(5)]
    for group in range(24):
        sums = [None] * 5
        for chunk in range(8):
            owner, tile = owner_and_tile(group, chunk)
            values = tile_ref[owner, tile]
            lanes = slice(128 * chunk, 128 * chunk + 128)
            others = [
                weight_ref[breadth * j + 8 * group : breadth * j + 8 * group + 8, lanes] for j in range(3)
            ] + [edge_ref[0:8, lanes], edge_ref[8:16, lanes]]
            for j, other in enumerate(others):
                product = values * other
                sums[j] = product if sums[j] is None else sums[j] + product
        for j in range(5):
            totals[j].append(sums[j])
    lanes = lax.broadcasted_iota(jnp.int32, (breadth, 128), 1)
    small = small_in_ref[...]
    for j in range(5):
        total = jnp.sum(jnp.concatenate(totals[j], axis=0), axis=1, keepdims=True)
        if j >= 3:
            total = total * ends_ref[:, j - 3 : j - 2]
        small = small + jnp.where(lanes == 5 + j, total, 0.0)
    rows = small.T
    tail = jnp.concatenate([rows[0:5, 128:192], rows[5:10, 128:192]], axis=1)
    packed = jnp.concatenate([rows[0:10, 0:128], tail, jnp.zeros((1, 128), jnp.float32)], axis=0)
    for block in range(BLOCKS):
        send_ref[block] = packed


def make_send(tiles, weights, ends, edges, small):
    return pl.pallas_call(
        send_kernel,
        out_shape=jax.ShapeDtypeStruct((BLOCKS, 16, 128), jnp.float32),
        in_specs=[pl.BlockSpec()] * 5,
        out_specs=pl.BlockSpec(),
        compiler_params=pltpu.CompilerParams(vmem_limit_bytes=VMEM_LIMIT),
        cost_estimate=pl.CostEstimate(flops=2_000_000, bytes_accessed=4_000_000, transcendentals=0),
        name="make_send",
    )(tiles, weights, ends, edges, small)


def inside_kernel(
    halo_ref, column_ref, tile_hbm, block_hbm, signal_hbm, query_hbm,
    out_hbm, self_ref, partner_ref,
    tile_ref, block_ref, signal_ref, query_ref, level_ref, gated_ref, sem,
):
    get_tiles = pltpu.make_async_copy(tile_hbm, tile_ref, sem.at[0])
    get_signal = pltpu.make_async_copy(signal_hbm, signal_ref, sem.at[1])
    get_query = pltpu.make_async_copy(query_hbm, query_ref, sem.at[2])
    get_block = strips(block_hbm.at[0], block_ref, sem, 3, 1)
    get_tiles.start()
    for copy in get_block:
        copy.start()
    get_signal.start()
    get_query.start()
    get_tiles.wait()
    unpack(tile_ref, level_ref, 0)
    left = split_two(level_ref[...])
    for at in range(4):
        part = slice(256 * at, 256 * at + 256)
        get_block[at].wait()
        gated_ref[:, part] = dot_three(left, split_two(block_ref[:, part]), 1, 0)
    get_signal.wait()
    get_query.wait()
    values, gated = signal_ref[...], gated_ref[...]
    prev, later = shifted(values, halo_ref[:, 0:1], halo_ref[:, 1:2])
    total = gated * conv(column_ref, 3, prev, values, later)
    for rows, tap in ((query_ref[...], 0), (gated * values, 3)):
        behind, ahead = shifted(rows, 0.0, 0.0)
        total = total + conv(column_ref, tap, ahead, rows, behind)
    level_ref[...] = total
    put = pltpu.make_async_copy(level_ref, out_hbm, sem.at[7])
    put.start()
    mix_ref = tile_ref.at[:, WEIGHT_TILE]
    mixes = []
    for group in range(16):
        mixes.append(mix_ref[2 * group] + mix_ref[2 * group + 1])
    for group in range(8):
        four = mix_ref[4 * group] + mix_ref[4 * group + 1] + mix_ref[4 * group + 2] + mix_ref[4 * group + 3]
        mixes.append(pltpu.roll(four, 64, 1))
    mixes = (jnp.concatenate(mixes, axis=0) * ROW_SCALE).T
    for section in range(SECTIONS):
        self_ref[section] = mixes[section : section + 1]
        partner_ref[section] = mixes[SECTIONS + section : SECTIONS + section + 1]
    put.wait()


def make_inside(tiles, block, signal, grad_query, halo, columns):
    mix = jax.ShapeDtypeStruct((SECTIONS, 1, signal.shape[0]), jnp.float32)
    buffer = pltpu.VMEM(signal.shape, jnp.float32)
    return pl.pallas_call(
        inside_kernel,
        out_shape=[jax.ShapeDtypeStruct(signal.shape, jnp.float32), mix, mix],
        in_specs=[pl.BlockSpec()] * 2 + [IN_HBM] * 4,
        out_specs=[IN_HBM] + [pl.BlockSpec()] * 2,
        scratch_shapes=[
            pltpu.VMEM(tiles.shape, jnp.float32),
            pltpu.VMEM(block.shape[1:], jnp.float32),
            buffer,
            buffer,
            buffer,
            buffer,
            pltpu.SemaphoreType.DMA((8,)),
        ],
        compiler_params=pltpu.CompilerParams(vmem_limit_bytes=VMEM_LIMIT),
        cost_estimate=pl.CostEstimate(flops=1_200_000_000, bytes_accessed=8_000_000, transcendentals=0),
        name="make_inside",
    )(halo, columns, tiles, block, signal, grad_query)


def edge_kernel(block_ref, got_ref, column_ref, in_ref, out_ref, tap_q_ref, tap_k_ref):
    at = pl.program_id(0)
    block = block_ref[0]

    def table(packed):
        low = packed[0:10]
        high = jnp.concatenate([packed[10:15, 0:64], packed[10:15, 64:128]], axis=0)
        return jnp.concatenate([low, high], axis=1)

    def columns(packed):
        rows = table(packed)
        return jnp.concatenate([rows, jnp.zeros((118, 192), jnp.float32)], axis=0).T

    source = jnp.where(at == 0, jnp.maximum(block - 1, 0), jnp.minimum(block + 1, BLOCKS - 1))
    inside = jnp.where(at == 0, block > 0, block < BLOCKS - 1)
    halo = jnp.where(inside, columns(got_ref[source]), 0.0)
    lanes = lax.broadcasted_iota(jnp.int32, (192, 128), 1)

    @pl.when(at == 0)
    def _():
        extra = column_ref[:, 2:3] * halo[:, 4:5] + column_ref[:, 5:6] * halo[:, 9:10]
        out_ref[...] = in_ref[...] + jnp.where(lanes == 0, extra, 0.0)
        sums = table(jnp.sum(got_ref[...], axis=0)) * TOKEN_SCALE
        tap_q_ref[...] = sums[0:3]
        tap_k_ref[...] = sums[5:8]

    @pl.when(at == 1)
    def _():
        extra = column_ref[:, 0:1] * halo[:, 3:4] + column_ref[:, 3:4] * halo[:, 8:9]
        out_ref[...] = in_ref[...] + jnp.where(lanes == 127, extra, 0.0)


def make_edges(block, got, columns, inside):
    whole = lambda shape: pl.BlockSpec(shape, lambda i: (0,) * len(shape))
    last = inside.shape[1] // 128 - 1
    strip = pl.BlockSpec((inside.shape[0], 128), lambda i: (0, last * i))
    return pl.pallas_call(
        edge_kernel,
        grid=(2,),
        out_shape=[
            jax.ShapeDtypeStruct(inside.shape, jnp.float32),
            jax.ShapeDtypeStruct((3, inside.shape[0]), jnp.float32),
            jax.ShapeDtypeStruct((3, inside.shape[0]), jnp.float32),
        ],
        in_specs=[
            pl.BlockSpec(memory_space=pltpu.SMEM),
            whole(got.shape),
            whole(columns.shape),
            strip,
        ],
        out_specs=[strip] + [whole((3, inside.shape[0]))] * 2,
        input_output_aliases={3: 0},
        compiler_params=pltpu.CompilerParams(vmem_limit_bytes=VMEM_LIMIT),
        cost_estimate=pl.CostEstimate(flops=200_000, bytes_accessed=900_000, transcendentals=0),
        name="make_edges",
    )(block, got, columns, inside)


def local(signal, cotangent, kernel_q, kernel_k, block_first, block_second, mix_self, mix_partner):
    before, after = neighbours(signal[-1:], signal[:1])
    signal, cotangent = signal.T, cotangent.T
    swap = lambda tiles: lax.all_to_all(tiles, "seq", 0, 0, tiled=True)
    after_both = lax.optimization_barrier
    place = lax.axis_index("ch").reshape(1)
    block = lax.axis_index("seq").reshape(1)

    packed, gated_in, grad_mixed, halo, columns = prologue(
        signal, cotangent, before, after, kernel_q, kernel_k, mix_self, mix_partner,
        block_first, block_second,
    )
    incoming = swap(packed)
    gated_other, mixed_other = other_core(gated_in), other_core(grad_mixed)
    level_last = swap(butterfly_forward(incoming))
    grad_tiles = butterfly_backward(incoming)
    tap_parts = tap_weights(signal, halo, block_first)
    level_last, grad_tiles, tap_parts = after_both((level_last, grad_tiles, tap_parts))
    returned = swap(grad_tiles)

    level_other = other_core(level_last)
    pieces = block_products(
        second_kernel, (384, 1024), "block_second_products", place,
        grad_mixed, mixed_other, level_last, level_other,
    )
    level_last, pieces = after_both((level_last, pieces))
    output, grad_query, small = make_output(
        level_last, block_second, cotangent, signal, columns, halo
    )
    second_received = receive_pieces(pieces)
    second_own = pieces[0]
    returned, small, second_received[1:] = after_both((returned, small, second_received[1:]))

    returned_other = other_core(returned)
    send = make_send(returned, *tap_parts, small)
    returned_other, send = after_both((returned_other, send))
    pieces = first_products(place, returned, returned_other, gated_in, gated_other)
    first_received = receive_pieces(pieces)
    send, pieces = after_both((send, pieces))
    got = swap(send)
    inside, mix_self_grad, mix_partner_grad = make_inside(
        returned, block_first, signal, grad_query, halo, columns
    )
    grad_second = second_own + second_received[0] + second_received[1] + second_received[2]
    grad_signal, tap_q_grad, tap_k_grad = make_edges(block, got, columns, inside)
    grad_first = pieces[0] + first_received[0] + first_received[1] + first_received[2]

    return (
        output.T,
        grad_signal.T,
        tap_q_grad,
        tap_k_grad,
        grad_first[None],
        grad_second[None],
        mix_self_grad,
        mix_partner_grad,
    )


def solution(mesh):
    return jax.shard_map(
        local,
        mesh=mesh,
        in_specs=(
            P("seq", "ch"),
            P("seq", "ch"),
            P(None, "ch"),
            P(None, "ch"),
            P("seq", None, None),
            P("seq", None, None),
            P(None, "seq", "ch"),
            P(None, "seq", "ch"),
        ),
        out_specs=(
            P("seq", "ch"),
            P("seq", "ch"),
            P(None, "ch"),
            P(None, "ch"),
            P("seq", "ch", None),
            P("seq", "ch", None),
            P(None, "seq", "ch"),
            P(None, "seq", "ch"),
        ),
        check_vma=False,
    )
```

profile of v0, /device:TPU:6, one launch (start us, length us, event | category | flops | bytes accessed | tf_op | source)
XLA Modules:
  0.0 176.4 jit_solution(7590032533951698780)
XLA Ops:
  0.6 1.0 fusion
  1.7 0.1 copy.19
  1.7 3.5 %collective-permute-start = (f32[1,192]{1,0:T(1,128)S(1)}, f32[1,192]{1,0:T(1,128)S(1)}, u32[]{:S(2)}, u32[]{:S(2)}) collective-permute-start(f32[1,192]{1,0:T(1,128)S(1)} %copy.19), channel_id=1, source_target_pairs={{0,8},{8,16},{16,24},{24,32},{32,40},{40,48},{48,56},{56,64},{64,7... | collective-permute-start | bytes 2312 | tf_op jit(solution)/shard_map/ppermute | solution.py:141
  5.2 0.1 copy.20
  5.3 1.3 collective-permute-start.1
  6.6 0.0 collective-permute-done.before_ref
  6.6 0.0 copy-start.5
  6.6 4.1 %collective-permute-done.1.after_ref = f32[1,192]{1,0:T(1,128)S(1)} collective-permute-done((f32[1,192]{1,0:T(1,128)S(1)}, f32[1,192]{1,0:T(1,128)S(1)}, u32[]{:S(2)}, u32[]{:S(2)}) %collective-permute-start.1) | collective-permute-done | bytes 800 | tf_op jit(solution)/shard_map/ppermute | solution.py:142
  10.8 0.0 copy-start.6
  10.8 0.0 copy-done.5
  10.8 0.6 copy-done.6
  11.3 9.3 %prologue.1 = (f32[32,13,8,128]{3,2,1,0:T(8,128)}, f32[192,1024]{1,0:T(8,128)}, f32[192,1024]{1,0:T(8,128)}, f32[192,128]{1,0:T(8,128)}, f32[192,128]{1,0:T(8,128)}) custom-call(f32[192,1024]{1,0:T(8,128)} %bitcast.10, f32[192,1024]{1,0:T(8,128)} %bitcast.14, f32[1,192]{1,0:T(1,128)} %copy-done.5, f32[1,192]{1,0:T(1,128)} %copy-done.6, f32[3,192]{1,0:T(4,128)} %taps_q_ref.1, ...), custom_call_target="tpu_custom_call" | custom-call | flops 2400000000 | bytes 15000000 | tf_op jit(solution)/shard_map/prologue/pallas_call | solution.py:311
  20.7 54.8 %all_to_all.20.in_ref = f32[32,13,8,128]{3,2,1,0:T(8,128)S(1)} all-to-all(f32[32,13,8,128]{3,2,1,0:T(8,128)} %get-tuple-element.53), channel_id=1, replica_groups=mesh['seq'=32,'ch'=8] {'seq'}, dimensions={0} | all-to-all | bytes 3407872 | tf_op jit(solution)/shard_map/all_to_all | solution.py:672
  75.5 2.2 %butterfly_forward.1 = f32[32,6,8,128]{3,2,1,0:T(8,128)} custom-call(f32[32,13,8,128]{3,2,1,0:T(8,128)S(1)} %all_to_all.20.in_ref), custom_call_target="tpu_custom_call" | custom-call | flops 4000000 | bytes 1800000 | tf_op jit(solution)/shard_map/butterfly_forward/pallas_call | solution.py:110
  77.7 4.7 %all-to-all-start.1 = ((f32[32,6,8,128]{3,2,1,0:T(8,128)}), f32[32,6,8,128]{3,2,1,0:T(8,128)S(1)}, u32[]{:S(2)}, u32[]{:S(2)}) async-start(f32[32,6,8,128]{3,2,1,0:T(8,128)} %butterfly_forward.1), calls=%async_computation.1 | async-start | bytes 1572864 | tf_op jit(solution)/shard_map/all_to_all | solution.py:672
  82.4 7.9 %tap_weights.1 = (f32[576,1024]{1,0:T(8,128)}, f32[192,128]{1,0:T(8,128)}, f32[16,1024]{1,0:T(8,128)}) custom-call(f32[192,128]{1,0:T(8,128)} %get-tuple-element.52.halo_ref, f32[192,1024]{1,0:T(8,128)} %bitcast.11, f32[1,1024,1024]{2,1,0:T(8,128)} %block_hbm.3), custom_call_target="tpu_custom_call" | custom-call | flops 3600000000 | bytes 8000000 | tf_op jit(solution)/shard_map/tap_weights/pallas_call | solution.py:474
  90.4 0.0 copy-start.9
  90.4 4.0 %butterfly_backward.1 = f32[32,7,8,128]{3,2,1,0:T(8,128)} custom-call(f32[32,13,8,128]{3,2,1,0:T(8,128)S(1)} %all_to_all.20.in_ref), custom_call_target="tpu_custom_call" | custom-call | flops 12000000 | bytes 2600000 | tf_op jit(solution)/shard_map/butterfly_backward/pallas_call | solution.py:123
  94.3 9.8 %all-to-all-done.1.right_a.tile_hbm = f32[32,6,8,128]{3,2,1,0:T(8,128)S(1)} async-done(((f32[32,6,8,128]{3,2,1,0:T(8,128)}), f32[32,6,8,128]{3,2,1,0:T(8,128)S(1)}, u32[]{:S(2)}, u32[]{:S(2)}) %all-to-all-start.1) | async-done | bytes 786464 | tf_op jit(solution)/shard_map/all_to_all | solution.py:672
  104.1 0.0 copy-start.1
  104.1 4.8 %all-to-all-start.2 = ((f32[32,7,8,128]{3,2,1,0:T(8,128)}), f32[32,7,8,128]{3,2,1,0:T(8,128)S(1)}, u32[]{:S(2)}, u32[]{:S(2)}) async-start(f32[32,7,8,128]{3,2,1,0:T(8,128)} %butterfly_backward.1), calls=%async_computation.2 | async-start | bytes 1835008 | tf_op jit(solution)/shard_map/all_to_all | solution.py:672
  108.9 0.0 copy-done.9
  108.9 0.1 collective-permute-start.2
  109.0 0.5 collective-permute-start.3
  109.5 1.9 %collective-permute-done.2.left_b = f32[192,1024]{1,0:T(8,128)} collective-permute-done((f32[192,1024]{1,0:T(8,128)S(1)}, f32[192,1024]{1,0:T(8,128)}, u32[]{:S(2)}, u32[]{:S(2)}) %collective-permute-start.2) | collective-permute-done | bytes 786464 | tf_op jit(solution)/shard_map/ppermute | solution.py:352
  111.4 1.1 collective-permute-done.3.right_b
  112.5 0.0 copy-done.1
  112.6 4.5 %block_second_products.1 = (f32[128,1024]{1,0:T(8,128)}, f32[128,1024]{1,0:T(8,128)}, f32[128,1024]{1,0:T(8,128)}, f32[128,1024]{1,0:T(8,128)}) custom-call(s32[1]{0:T(128)} %bitcast.2.place_ref, f32[192,1024]{1,0:T(8,128)} %get-tuple-element.58.left_a, f32[192,1024]{1,0:T(8,128)} %collective-permute-done.2.left_b, f32[32,6,8,128]{3,2,1,0:T(8,128)} %copy-done.1, ...), custom_call_target="tpu_custom_call" | custom-call | flops 1200000000 | bytes 5000000 | tf_op jit(solution)/shard_map/block_second_products/pallas_call | solution.py:339
  117.0 0.5 collective-permute-start.4
  117.5 1.5 collective-permute-start.5
  119.1 0.0 copy-start.8
  119.1 8.8 %make_output.1 = (f32[192,1024]{1,0:T(8,128)}, f32[192,1024]{1,0:T(8,128)}, f32[192,128]{1,0:T(8,128)}) custom-call(f32[192,128]{1,0:T(8,128)} %get-tuple-element.51.column_ref, f32[192,128]{1,0:T(8,128)} %get-tuple-element.52.halo_ref, f32[32,6,8,128]{3,2,1,0:T(8,128)} %copy-done.1, f32[1,1024,1024]{2,1,0:T(8,128)} %block_hbm.2, f32[192,1024]{1,0:T(8,128)} %bitcast.12, ...), custom_call_target="tpu_custom_call" | custom-call | flops 1200000000 | bytes 9000000 | tf_op jit(solution)/shard_map/make_output/pallas_call | solution.py:428
  127.9 3.3 %collective-permute-done.4 = f32[128,1024]{1,0:T(8,128)S(1)} collective-permute-done((f32[128,1024]{1,0:T(8,128)}, f32[128,1024]{1,0:T(8,128)S(1)}, u32[]{:S(2)}, u32[]{:S(2)}) %collective-permute-start.4) | collective-permute-done | bytes 524320 | tf_op jit(solution)/shard_map/ppermute | solution.py:357
  131.2 1.5 collective-permute-done.5
  132.7 0.6 all-to-all-done.2.tile_ref.tiles_a.tile_hbm
  133.3 0.0 collective-permute-start.6
  133.3 0.0 copy-done.8
  133.3 0.5 collective-permute-start.7
  133.8 1.4 collective-permute-start.11
  135.2 0.0 copy-done
  135.2 3.3 %make_send.1 = f32[32,16,128]{2,1,0:T(8,128)} custom-call(f32[32,7,8,128]{3,2,1,0:T(8,128)} %copy-done, f32[576,1024]{1,0:T(8,128)} %get-tuple-element.70.weight_ref, f32[192,128]{1,0:T(8,128)} %get-tuple-element.71.ends_ref, f32[16,1024]{1,0:T(8,128)} %get-tuple-element.72.edge_ref, f32[192,128]{1,0:T(8,128)} %get-tuple-element.73.small_in_ref), custom_call_target="tpu_custom_call" | custom-call | flops 2000000 | bytes 4000000 | tf_op jit(solution)/shard_map/make_send/pallas_call | solution.py:531
  138.5 0.0 collective-permute-done.6.tiles_b
  138.5 0.0 collective-permute-done.7.right_b
  138.5 0.9 copy-done.7
  139.5 0.9 copy-done.10
  140.4 4.4 %block_first_products.1 = (f32[128,1024]{1,0:T(8,128)}, f32[128,1024]{1,0:T(8,128)}, f32[128,1024]{1,0:T(8,128)}, f32[128,1024]{1,0:T(8,128)}) custom-call(s32[1]{0:T(128)} %bitcast.2.place_ref, f32[32,7,8,128]{3,2,1,0:T(8,128)} %copy-done, f32[32,7,8,128]{3,2,1,0:T(8,128)} %copy-done.7, f32[192,1024]{1,0:T(8,128)} %get-tuple-element.76.right_a, ...), custom_call_target="tpu_custom_call" | custom-call | flops 1200000000 | bytes 5000000 | tf_op jit(solution)/shard_map/block_first_products/pallas_call | solution.py:218
  144.8 0.1 collective-permute-start.10
  144.9 3.6 %collective-permute-start.8 = (f32[128,1024]{1,0:T(8,128)}, f32[128,1024]{1,0:T(8,128)S(1)}, u32[]{:S(2)}, u32[]{:S(2)}) collective-permute-start(f32[128,1024]{1,0:T(8,128)} %get-tuple-element.79), channel_id=1, source_target_pairs={{0,4},{1,5},{2,6},{3,7},{4,0},{5,1},{6,2},{7,3},{8,12},{9,13},{10,... | collective-permute-start | bytes 1572872 | tf_op jit(solution)/shard_map/ppermute | solution.py:357
  148.5 1.2 collective-permute-start.9
  149.6 9.4 %all-to-all-start.3 = ((f32[32,16,128]{2,1,0:T(8,128)}), f32[32,16,128]{2,1,0:T(8,128)S(1)}, u32[]{:S(2)}, u32[]{:S(2)}) async-start(f32[32,16,128]{2,1,0:T(8,128)} %make_send.1), calls=%async_computation.3 | async-start | bytes 524288 | tf_op jit(solution)/shard_map/all_to_all | solution.py:672
  159.1 0.0 copy-start.3
  159.1 9.1 %make_inside.1 = (f32[192,1024]{1,0:T(8,128)}, f32[5,1,192]{2,1,0:T(1,128)}, f32[5,1,192]{2,1,0:T(1,128)}) custom-call(f32[192,128]{1,0:T(8,128)} %get-tuple-element.52.halo_ref, f32[192,128]{1,0:T(8,128)} %get-tuple-element.51.column_ref, f32[32,7,8,128]{3,2,1,0:T(8,128)} %copy-done, f32[1,1024,1024]{2,1,0:T(8,128)} %block_hbm.3, f32[192,1024]{1,0:T(8,128)} %bitcast.13, ...), custom_call_target="tpu_custom_call" | custom-call | flops 1200000000 | bytes 8000000 | tf_op jit(solution)/shard_map/make_inside/pallas_call | solution.py:591
  168.2 0.0 copy-start.4
  168.2 0.0 collective-permute-done.11
  168.2 0.0 copy-done.3
  168.2 0.9 add_bitcast_fusion
  169.2 2.0 %all-to-all-done.3.got_ref = f32[32,16,128]{2,1,0:T(8,128)S(1)} async-done(((f32[32,16,128]{2,1,0:T(8,128)}), f32[32,16,128]{2,1,0:T(8,128)S(1)}, u32[]{:S(2)}, u32[]{:S(2)}) %all-to-all-start.3) | async-done | bytes 262176 | tf_op jit(solution)/shard_map/all_to_all | solution.py:672
  171.2 0.7 copy-done.2
  171.9 2.5 %make_edges.1 = (f32[192,1024]{1,0:T(8,128)}, f32[3,192]{1,0:T(4,128)}, f32[3,192]{1,0:T(4,128)}) custom-call(s32[1]{0:T(128)} %bitcast.4.block_ref, f32[32,16,128]{2,1,0:T(8,128)} %copy-done.2, f32[192,128]{1,0:T(8,128)} %get-tuple-element.51.column_ref, f32[192,1024]{1,0:T(8,128)} %get-tuple-element.83.in_ref), custom_call_target="tpu_custom_call", output_to_operand_aliasing={{0}: (3, {})} | custom-call | flops 200000 | bytes 900000 | tf_op jit(solution)/shard_map/make_edges/pallas_call | solution.py:647
  174.4 0.0 collective-permute-done.10
  174.4 0.0 collective-permute-done.8
  174.4 0.0 collective-permute-done.9
  174.4 0.0 copy-done.4
  174.4 2.0 %add_bitcast_fusion.1 = f32[1,128,1024]{2,1,0:T(8,128)} fusion(f32[128,1024]{1,0:T(8,128)S(1)} %collective-permute-done.10, f32[128,1024]{1,0:T(8,128)} %collective-permute-done.9, f32[128,1024]{1,0:T(8,128)S(1)} %copy-done.4, f32[128,1024]{1,0:T(8,128)S(1)} %collective-permute-done.8), kind=kLoop, calls=%fused_computation.1 | loop fusion | flops 393216 | bytes 2621440 | tf_op jit(solution)/shard_map/broadcast_in_dim | solution.py:721
  (4 shorter events, 0.0 us)
Async XLA Ops:
  1.7 4.9 %collective-permute-start = (f32[1,192]{1,0:T(1,128)S(1)}, f32[1,192]{1,0:T(1,128)S(1)}, u32[]{:S(2)}, u32[]{:S(2)}) collective-permute-start(f32[1,192]{1,0:T(1,128)S(1)} %copy.19), channel_id=1, source_target_pairs={{0,8},{8,16},{16,24},{24,32},{32,40},{40,48},{48,56},{56,64},{64,7... | collective-permute-start | bytes 2312 | tf_op jit(solution)/shard_map/ppermute | solution.py:141
  5.3 5.5 %collective-permute-start.1 = (f32[1,192]{1,0:T(1,128)S(1)}, f32[1,192]{1,0:T(1,128)S(1)}, u32[]{:S(2)}, u32[]{:S(2)}) collective-permute-start(f32[1,192]{1,0:T(1,128)S(1)} %copy.20), channel_id=1, source_target_pairs={{8,0},{16,8},{24,16},{32,24},{40,32},{48,40},{56,48},{64,56},{72,6... | collective-permute-start | bytes 2312 | tf_op jit(solution)/shard_map/ppermute | solution.py:142
  6.6 4.2 %copy-start.5 = (f32[1,192]{1,0:T(1,128)}, f32[1,192]{1,0:T(1,128)S(1)}, u32[]{:S(2)}) copy-start(f32[1,192]{1,0:T(1,128)S(1)} %collective-permute-done.before_ref) | copy-start | bytes 2308
  10.8 0.6 copy-start.6
  77.7 26.5 %all-to-all-start.1 = ((f32[32,6,8,128]{3,2,1,0:T(8,128)}), f32[32,6,8,128]{3,2,1,0:T(8,128)S(1)}, u32[]{:S(2)}, u32[]{:S(2)}) async-start(f32[32,6,8,128]{3,2,1,0:T(8,128)} %butterfly_forward.1), calls=%async_computation.1 | async-start | bytes 1572864 | tf_op jit(solution)/shard_map/all_to_all | solution.py:672
  90.4 18.5 %copy-start.9 = (f32[192,1024]{1,0:T(8,128)S(1)}, f32[192,1024]{1,0:T(8,128)}, u32[]{:S(2)}) copy-start(f32[192,1024]{1,0:T(8,128)} %get-tuple-element.58.left_a) | copy-start | bytes 2359300
  104.1 8.4 %copy-start.1 = (f32[32,6,8,128]{3,2,1,0:T(8,128)}, f32[32,6,8,128]{3,2,1,0:T(8,128)S(1)}, u32[]{:S(2)}) copy-start(f32[32,6,8,128]{3,2,1,0:T(8,128)S(1)} %all-to-all-done.1.right_a.tile_hbm) | copy-start | bytes 2359300
  104.1 29.2 %all-to-all-start.2 = ((f32[32,7,8,128]{3,2,1,0:T(8,128)}), f32[32,7,8,128]{3,2,1,0:T(8,128)S(1)}, u32[]{:S(2)}, u32[]{:S(2)}) async-start(f32[32,7,8,128]{3,2,1,0:T(8,128)} %butterfly_backward.1), calls=%async_computation.2 | async-start | bytes 1835008 | tf_op jit(solution)/shard_map/all_to_all | solution.py:672
  108.9 2.5 %collective-permute-start.2 = (f32[192,1024]{1,0:T(8,128)S(1)}, f32[192,1024]{1,0:T(8,128)}, u32[]{:S(2)}, u32[]{:S(2)}) collective-permute-start(f32[192,1024]{1,0:T(8,128)S(1)} %copy-done.9), channel_id=1, source_target_pairs={{0,1},{1,0},{2,3},{3,2},{4,5},{5,4},{6,7},{7,6},{8,9},{9,8},{10,11... | collective-permute-start | bytes 2359304 | tf_op jit(solution)/shard_map/ppermute | solution.py:352
  109.0 3.5 %collective-permute-start.3 = (f32[32,6,8,128]{3,2,1,0:T(8,128)S(1)}, f32[32,6,8,128]{3,2,1,0:T(8,128)}, u32[]{:S(2)}, u32[]{:S(2)}) collective-permute-start(f32[32,6,8,128]{3,2,1,0:T(8,128)S(1)} %all-to-all-done.1.right_a.tile_hbm), channel_id=1, source_target_pairs={{0,1},{1,0},{2,3},{3,2},{4,5},{5,4},{6,7},{7,6},{8,9},{9,8},{10,11... | collective-permute-start | bytes 2359304 | tf_op jit(solution)/shard_map/ppermute | solution.py:352
  117.0 14.2 %collective-permute-start.4 = (f32[128,1024]{1,0:T(8,128)}, f32[128,1024]{1,0:T(8,128)S(1)}, u32[]{:S(2)}, u32[]{:S(2)}) collective-permute-start(f32[128,1024]{1,0:T(8,128)} %get-tuple-element.67), channel_id=1, source_target_pairs={{0,2},{1,3},{2,4},{3,5},{4,6},{5,7},{6,0},{7,1},{8,10},{9,11},{10,... | collective-permute-start | bytes 1572872 | tf_op jit(solution)/shard_map/ppermute | solution.py:357
  117.5 15.2 %collective-permute-start.5 = (f32[128,1024]{1,0:T(8,128)}, f32[128,1024]{1,0:T(8,128)S(1)}, u32[]{:S(2)}, u32[]{:S(2)}) collective-permute-start(f32[128,1024]{1,0:T(8,128)} %get-tuple-element.68), channel_id=1, source_target_pairs={{0,6},{1,7},{2,0},{3,1},{4,2},{5,3},{6,4},{7,5},{8,14},{9,15},{10,... | collective-permute-start | bytes 1572872 | tf_op jit(solution)/shard_map/ppermute | solution.py:357
  119.1 14.2 %copy-start.8 = (f32[192,1024]{1,0:T(8,128)S(1)}, f32[192,1024]{1,0:T(8,128)}, u32[]{:S(2)}) copy-start(f32[192,1024]{1,0:T(8,128)} %get-tuple-element.76.right_a) | copy-start | bytes 2359300
  133.3 1.9 %copy-start = (f32[32,7,8,128]{3,2,1,0:T(8,128)}, f32[32,7,8,128]{3,2,1,0:T(8,128)S(1)}, u32[]{:S(2)}) copy-start(f32[32,7,8,128]{3,2,1,0:T(8,128)S(1)} %all-to-all-done.2.tile_ref.tiles_a.tile_hbm) | copy-start | bytes 2752516
  133.3 5.2 %collective-permute-start.6 = (f32[32,7,8,128]{3,2,1,0:T(8,128)S(1)}, f32[32,7,8,128]{3,2,1,0:T(8,128)S(1)}, u32[]{:S(2)}, u32[]{:S(2)}) collective-permute-start(f32[32,7,8,128]{3,2,1,0:T(8,128)S(1)} %all-to-all-done.2.tile_ref.tiles_a.tile_hbm), channel_id=1, source_target_pairs={{0,1},{1,0},{2,3},{3,2},{4,5},{5,4},{6,7},{7,6},{8,9},{9,8},{10,11... | collective-permute-start | bytes 2752520 | tf_op jit(solution)/shard_map/ppermute | solution.py:352
  133.3 5.2 %collective-permute-start.7 = (f32[192,1024]{1,0:T(8,128)S(1)}, f32[192,1024]{1,0:T(8,128)S(1)}, u32[]{:S(2)}, u32[]{:S(2)}) collective-permute-start(f32[192,1024]{1,0:T(8,128)S(1)} %copy-done.8), channel_id=1, source_target_pairs={{0,1},{1,0},{2,3},{3,2},{4,5},{5,4},{6,7},{7,6},{8,9},{9,8},{10,11... | collective-permute-start | bytes 2359304 | tf_op jit(solution)/shard_map/ppermute | solution.py:352
  133.8 34.4 %collective-permute-start.11 = (f32[128,1024]{1,0:T(8,128)}, f32[128,1024]{1,0:T(8,128)S(1)}, u32[]{:S(2)}, u32[]{:S(2)}) collective-permute-start(f32[128,1024]{1,0:T(8,128)} %get-tuple-element.89), channel_id=1, source_target_pairs={{0,4},{1,5},{2,6},{3,7},{4,0},{5,1},{6,2},{7,3},{8,12},{9,13},{10,... | collective-permute-start | bytes 1572872 | tf_op jit(solution)/shard_map/ppermute | solution.py:357
  138.5 0.9 copy-start.7
  139.5 0.9 copy-start.10
  144.8 29.6 %collective-permute-start.10 = (f32[128,1024]{1,0:T(8,128)}, f32[128,1024]{1,0:T(8,128)S(1)}, u32[]{:S(2)}, u32[]{:S(2)}) collective-permute-start(f32[128,1024]{1,0:T(8,128)} %get-tuple-element.80), channel_id=1, source_target_pairs={{0,6},{1,7},{2,0},{3,1},{4,2},{5,3},{6,4},{7,5},{8,14},{9,15},{10,... | collective-permute-start | bytes 1572872 | tf_op jit(solution)/shard_map/ppermute | solution.py:357
  144.9 29.5 %collective-permute-start.8 = (f32[128,1024]{1,0:T(8,128)}, f32[128,1024]{1,0:T(8,128)S(1)}, u32[]{:S(2)}, u32[]{:S(2)}) collective-permute-start(f32[128,1024]{1,0:T(8,128)} %get-tuple-element.79), channel_id=1, source_target_pairs={{0,4},{1,5},{2,6},{3,7},{4,0},{5,1},{6,2},{7,3},{8,12},{9,13},{10,... | collective-permute-start | bytes 1572872 | tf_op jit(solution)/shard_map/ppermute | solution.py:357
  148.5 25.9 %collective-permute-start.9 = (f32[128,1024]{1,0:T(8,128)}, f32[128,1024]{1,0:T(8,128)}, u32[]{:S(2)}, u32[]{:S(2)}) collective-permute-start(f32[128,1024]{1,0:T(8,128)} %get-tuple-element.78), channel_id=1, source_target_pairs={{0,2},{1,3},{2,4},{3,5},{4,6},{5,7},{6,0},{7,1},{8,10},{9,11},{10,... | collective-permute-start | bytes 1572872 | tf_op jit(solution)/shard_map/ppermute | solution.py:357
  149.6 21.5 %all-to-all-start.3 = ((f32[32,16,128]{2,1,0:T(8,128)}), f32[32,16,128]{2,1,0:T(8,128)S(1)}, u32[]{:S(2)}, u32[]{:S(2)}) async-start(f32[32,16,128]{2,1,0:T(8,128)} %make_send.1), calls=%async_computation.3 | async-start | bytes 524288 | tf_op jit(solution)/shard_map/all_to_all | solution.py:672
  159.1 9.2 %copy-start.3 = (f32[128,1024]{1,0:T(8,128)S(1)}, f32[128,1024]{1,0:T(8,128)}, u32[]{:S(2)}) copy-start(f32[128,1024]{1,0:T(8,128)} %get-tuple-element.88) | copy-start | bytes 1572868
  168.2 6.2 %copy-start.4 = (f32[128,1024]{1,0:T(8,128)S(1)}, f32[128,1024]{1,0:T(8,128)}, u32[]{:S(2)}) copy-start(f32[128,1024]{1,0:T(8,128)} %get-tuple-element.87) | copy-start | bytes 1572868
  171.2 0.7 copy-start.2
where the time goes:
time: 178 us; the launch traced here: 176 us
  Pallas kernels  56.1 us (32%)
  blocking collectives  54.8 us (31%)
  starting transfers between devices  33 us (19%)
  waiting for transfers between devices  24.4 us (14%)
  local copies, waits for them, and re-layouts  4.29 us (2%)
  other arithmetic  2.92 us (2%)
    all_to_all x1, blocking collectives, local(): swap = lambda tiles: lax.all_to_all(tiles, 'seq', 0, 0, tiled=True)  54.8 us
    all_to_all x3, starting transfers between devices, local(): swap = lambda tiles: lax.all_to_all(tiles, 'seq', 0, 0, tiled=True)  18.9 us
    all_to_all x3, waiting for transfers between devices, local(): swap = lambda tiles: lax.all_to_all(tiles, 'seq', 0, 0, tiled=True)  12.4 us
    pallas_call x1, Pallas kernels, prologue(): pl.pallas_call(prologue_kernel, grid=(height // COLUMNS,), out_shape=[jax...  9.34 us
    pallas_call x1, Pallas kernels, make_inside(): pl.pallas_call(inside_kernel, out_shape=[jax.ShapeDtypeStruct(signal.shap...  9.12 us
    pallas_call x1, Pallas kernels, make_output(): pl.pallas_call(output_kernel, out_shape=[full, full, jax.ShapeDtypeStruct...  8.83 us
    ppermute x6, starting transfers between devices, receive_pieces(): lax.ppermute(pieces[step], 'ch', [(i, (i + 2 * step) % (2 * CHIPS)) for i...  8.26 us
    pallas_call x1, Pallas kernels, tap_weights(): pl.pallas_call(tap_kernel, grid=(height // COLUMNS,), out_shape=[jax.Shap...  7.94 us
  transfers between devices with their start and end apart: 15, of which 8 were waited for; matrix products, arithmetic and copies ran while one was open for 1% of the time, Pallas kernels for 25%

commit v1 on v0

--- a/solution.py
+++ b/solution.py
@@ -411,13 +411,18 @@
         out_ref[:, part] = query[:, part] * mixed
         grad = cot_ref[:, part] * mixed
         grad_ref[:, part] = grad
-        for index, (ref, hbm) in enumerate(((out_ref, out_hbm), (grad_ref, grad_hbm))):
-            put = pltpu.make_async_copy(ref.at[:, part], hbm.at[:, part], sem.at[7 + 2 * at + index])
-            put.start()
-            puts.append(put)
+        put = pltpu.make_async_copy(out_ref.at[:, part], out_hbm.at[:, part], sem.at[7 + at])
+        put.start()
+        puts.append(put)
         new = tap_products(grad, prev[:, part], values[:, part], later[:, part])
         sums = new if sums is None else [a + b for a, b in zip(sums, new)]
     small_ref[...] = small_columns(sums, grad_ref[:, 0:1], grad_ref[:, 1023:1024], 0)
+    rows = grad_ref[...]
+    behind, ahead = shifted(rows, 0.0, 0.0)
+    level_ref[...] = conv(column_ref, 0, ahead, rows, behind)
+    put = pltpu.make_async_copy(level_ref, grad_hbm, sem.at[11])
+    put.start()
+    puts.append(put)
     for put in puts:
         put.wait()
 
@@ -438,7 +443,7 @@
             buffer,
             buffer,
             buffer,
-            pltpu.SemaphoreType.DMA((15,)),
+            pltpu.SemaphoreType.DMA((12,)),
         ],
         compiler_params=pltpu.CompilerParams(vmem_limit_bytes=VMEM_LIMIT),
         cost_estimate=pl.CostEstimate(flops=1_200_000_000, bytes_accessed=9_000_000, transcendentals=0),
@@ -565,9 +570,9 @@
     values, gated = signal_ref[...], gated_ref[...]
     prev, later = shifted(values, halo_ref[:, 0:1], halo_ref[:, 1:2])
     total = gated * conv(column_ref, 3, prev, values, later)
-    for rows, tap in ((query_ref[...], 0), (gated * values, 3)):
-        behind, ahead = shifted(rows, 0.0, 0.0)
-        total = total + conv(column_ref, tap, ahead, rows, behind)
+    rows = gated * values
+    behind, ahead = shifted(rows, 0.0, 0.0)
+    total = total + query_ref[...] + conv(column_ref, 3, ahead, rows, behind)
     level_ref[...] = total
     put = pltpu.make_async_copy(level_ref, out_hbm, sem.at[7])
     put.start()
@@ -683,7 +688,9 @@
     level_last = swap(butterfly_forward(incoming))
     grad_tiles = butterfly_backward(incoming)
     tap_parts = tap_weights(signal, halo, block_first)
-    level_last, grad_tiles, tap_parts = after_both((level_last, grad_tiles, tap_parts))
+    level_last, grad_tiles, tap_parts, gated_other, mixed_other = after_both(
+        (level_last, grad_tiles, tap_parts, gated_other, mixed_other)
+    )
     returned = swap(grad_tiles)
 
     level_other = other_core(level_last)

time: 178 us -> 174 us (0.978)
  waiting for transfers between devices: 24.4 us -> 22.2 us
  starting transfers between devices: 33 us -> 31 us
  transfers between devices with their start and end apart: 15 -> 15, of which waited for: 8 -> 8; matrix products, arithmetic and copies ran while one was open for 1% -> 1% of each run, Pallas kernels for 25% -> 26%
where the time goes in v1:
time: 174 us; the launch traced here: 173 us
  Pallas kernels  56.1 us (32%)
  blocking collectives  54.8 us (31%)
  starting transfers between devices  31 us (18%)
  waiting for transfers between devices  22.2 us (13%)
  local copies, waits for them, and re-layouts  5.15 us (3%)
  other arithmetic  2.97 us (2%)
    all_to_all x1, blocking collectives, local(): swap = lambda tiles: lax.all_to_all(tiles, 'seq', 0, 0, tiled=True)  54.8 us
    all_to_all x3, starting transfers between devices, local(): swap = lambda tiles: lax.all_to_all(tiles, 'seq', 0, 0, tiled=True)  18.5 us
    all_to_all x3, waiting for transfers between devices, local(): swap = lambda tiles: lax.all_to_all(tiles, 'seq', 0, 0, tiled=True)  11.1 us
    pallas_call x1, Pallas kernels, make_output(): pl.pallas_call(output_kernel, out_shape=[full, full, jax.ShapeDtypeStruct...  9.5 us
    pallas_call x1, Pallas kernels, prologue(): pl.pallas_call(prologue_kernel, grid=(height // COLUMNS,), out_shape=[jax...  9.34 us
    pallas_call x1, Pallas kernels, make_inside(): pl.pallas_call(inside_kernel, out_shape=[jax.ShapeDtypeStruct(signal.shap...  8.43 us
    pallas_call x1, Pallas kernels, tap_weights(): pl.pallas_call(tap_kernel, grid=(height // COLUMNS,), out_shape=[jax.Shap...  7.92 us
    ppermute x6, starting transfers between devices, receive_pieces(): lax.ppermute(pieces[step], 'ch', [(i, (i + 2 * step) % (2 * CHIPS)) for i...  7.05 us
  transfers between devices with their start and end apart: 15, of which 8 were waited for; matrix products, arithmetic and copies ran while one was open for 1% of the time, Pallas kernels for 26%

profile of v1, /device:TPU:6, one launch (start us, length us, event | category | flops | bytes accessed | tf_op | source)
XLA Modules:
  0.0 173.1 jit_solution(3877469518606632219)
XLA Ops:
  0.6 1.0 fusion
  1.7 0.1 copy.19
  1.7 3.5 %collective-permute-start = (f32[1,192]{1,0:T(1,128)S(1)}, f32[1,192]{1,0:T(1,128)S(1)}, u32[]{:S(2)}, u32[]{:S(2)}) collective-permute-start(f32[1,192]{1,0:T(1,128)S(1)} %copy.19), channel_id=1, source_target_pairs={{0,8},{8,16},{16,24},{24,32},{32,40},{40,48},{48,56},{56,64},{64,7... | collective-permute-start | bytes 2312 | tf_op jit(solution)/shard_map/ppermute | solution.py:141
  5.2 0.1 copy.20
  5.3 1.3 collective-permute-start.1
  6.6 0.0 collective-permute-done.before_ref
  6.6 0.0 copy-start.5
  6.6 4.1 %collective-permute-done.1.after_ref = f32[1,192]{1,0:T(1,128)S(1)} collective-permute-done((f32[1,192]{1,0:T(1,128)S(1)}, f32[1,192]{1,0:T(1,128)S(1)}, u32[]{:S(2)}, u32[]{:S(2)}) %collective-permute-start.1) | collective-permute-done | bytes 800 | tf_op jit(solution)/shard_map/ppermute | solution.py:142
  10.8 0.0 copy-start.6
  10.8 0.0 copy-done.5
  10.8 0.6 copy-done.6
  11.3 9.3 %prologue.1 = (f32[32,13,8,128]{3,2,1,0:T(8,128)}, f32[192,1024]{1,0:T(8,128)}, f32[192,1024]{1,0:T(8,128)}, f32[192,128]{1,0:T(8,128)}, f32[192,128]{1,0:T(8,128)}) custom-call(f32[192,1024]{1,0:T(8,128)} %bitcast.10, f32[192,1024]{1,0:T(8,128)} %bitcast.14, f32[1,192]{1,0:T(1,128)} %copy-done.5, f32[1,192]{1,0:T(1,128)} %copy-done.6, f32[3,192]{1,0:T(4,128)} %taps_q_ref.1, ...), custom_call_target="tpu_custom_call" | custom-call | flops 2400000000 | bytes 15000000 | tf_op jit(solution)/shard_map/prologue/pallas_call | solution.py:311
  20.7 54.8 %all_to_all.20.in_ref = f32[32,13,8,128]{3,2,1,0:T(8,128)S(1)} all-to-all(f32[32,13,8,128]{3,2,1,0:T(8,128)} %get-tuple-element.55), channel_id=1, replica_groups=mesh['seq'=32,'ch'=8] {'seq'}, dimensions={0} | all-to-all | bytes 3407872 | tf_op jit(solution)/shard_map/all_to_all | solution.py:677
  75.5 0.0 copy-start.8
  75.5 2.3 %butterfly_forward.1 = f32[32,6,8,128]{3,2,1,0:T(8,128)} custom-call(f32[32,13,8,128]{3,2,1,0:T(8,128)S(1)} %all_to_all.20.in_ref), custom_call_target="tpu_custom_call" | custom-call | flops 4000000 | bytes 1800000 | tf_op jit(solution)/shard_map/butterfly_forward/pallas_call | solution.py:110
  77.7 4.7 %all-to-all-start.1 = ((f32[32,6,8,128]{3,2,1,0:T(8,128)}), f32[32,6,8,128]{3,2,1,0:T(8,128)S(1)}, u32[]{:S(2)}, u32[]{:S(2)}) async-start(f32[32,6,8,128]{3,2,1,0:T(8,128)} %butterfly_forward.1), calls=%async_computation.1 | async-start | bytes 1572864 | tf_op jit(solution)/shard_map/all_to_all | solution.py:677
  82.5 0.0 copy-done.8
  82.5 0.1 collective-permute-start.2
  82.6 0.5 collective-permute-start.3
  83.1 7.9 %tap_weights.1 = (f32[576,1024]{1,0:T(8,128)}, f32[192,128]{1,0:T(8,128)}, f32[16,1024]{1,0:T(8,128)}) custom-call(f32[192,128]{1,0:T(8,128)} %get-tuple-element.54.halo_ref, f32[192,1024]{1,0:T(8,128)} %bitcast.11, f32[1,1024,1024]{2,1,0:T(8,128)} %block_hbm.3), custom_call_target="tpu_custom_call" | custom-call | flops 3600000000 | bytes 8000000 | tf_op jit(solution)/shard_map/tap_weights/pallas_call | solution.py:479
  91.0 4.0 %butterfly_backward.1 = f32[32,7,8,128]{3,2,1,0:T(8,128)} custom-call(f32[32,13,8,128]{3,2,1,0:T(8,128)S(1)} %all_to_all.20.in_ref), custom_call_target="tpu_custom_call" | custom-call | flops 12000000 | bytes 2600000 | tf_op jit(solution)/shard_map/butterfly_backward/pallas_call | solution.py:123
  95.0 0.0 collective-permute-done.2.right_b
  95.0 0.0 copy-start.9
  95.0 0.9 copy-done.9
  95.9 0.0 collective-permute-done.3.left_b
  95.9 8.4 %all-to-all-done.1.right_a.tile_hbm = f32[32,6,8,128]{3,2,1,0:T(8,128)S(1)} async-done(((f32[32,6,8,128]{3,2,1,0:T(8,128)}), f32[32,6,8,128]{3,2,1,0:T(8,128)S(1)}, u32[]{:S(2)}, u32[]{:S(2)}) %all-to-all-start.1) | async-done | bytes 786464 | tf_op jit(solution)/shard_map/all_to_all | solution.py:677
  104.2 0.0 copy-start.1
  104.2 4.8 %all-to-all-start.2 = ((f32[32,7,8,128]{3,2,1,0:T(8,128)}), f32[32,7,8,128]{3,2,1,0:T(8,128)S(1)}, u32[]{:S(2)}, u32[]{:S(2)}) async-start(f32[32,7,8,128]{3,2,1,0:T(8,128)} %butterfly_backward.1), calls=%async_computation.2 | async-start | bytes 1835008 | tf_op jit(solution)/shard_map/all_to_all | solution.py:677
  109.0 0.1 collective-permute-start.4
  109.1 2.3 %collective-permute-done.4.right_b = f32[32,6,8,128]{3,2,1,0:T(8,128)S(1)} collective-permute-done((f32[32,6,8,128]{3,2,1,0:T(8,128)S(1)}, f32[32,6,8,128]{3,2,1,0:T(8,128)S(1)}, u32[]{:S(2)}, u32[]{:S(2)}) %collective-permute-start.4) | collective-permute-done | bytes 786464 | tf_op jit(solution)/shard_map/ppermute | solution.py:352
  111.4 0.0 copy-done.1
  111.4 0.9 copy-done.10
  112.2 4.5 %block_second_products.1 = (f32[128,1024]{1,0:T(8,128)}, f32[128,1024]{1,0:T(8,128)}, f32[128,1024]{1,0:T(8,128)}, f32[128,1024]{1,0:T(8,128)}) custom-call(s32[1]{0:T(128)} %bitcast.2.place_ref, f32[192,1024]{1,0:T(8,128)} %get-tuple-element.60.left_a, f32[192,1024]{1,0:T(8,128)} %collective-permute-done.3.left_b, f32[32,6,8,128]{3,2,1,0:T(8,128)} %copy-done.1, ...), custom_call_target="tpu_custom_call" | custom-call | flops 1200000000 | bytes 5000000 | tf_op jit(solution)/shard_map/block_second_products/pallas_call | solution.py:339
  116.7 0.5 collective-permute-start.5
  117.2 1.5 collective-permute-start.6
  118.8 9.5 %make_output.1 = (f32[192,1024]{1,0:T(8,128)}, f32[192,1024]{1,0:T(8,128)}, f32[192,128]{1,0:T(8,128)}) custom-call(f32[192,128]{1,0:T(8,128)} %get-tuple-element.53.column_ref, f32[192,128]{1,0:T(8,128)} %get-tuple-element.54.halo_ref, f32[32,6,8,128]{3,2,1,0:T(8,128)} %copy-done.1, f32[1,1024,1024]{2,1,0:T(8,128)} %block_hbm.2, f32[192,1024]{1,0:T(8,128)} %bitcast.12, ...), custom_call_target="tpu_custom_call" | custom-call | flops 1200000000 | bytes 9000000 | tf_op jit(solution)/shard_map/make_output/pallas_call | solution.py:433
  128.3 2.7 %collective-permute-done.5 = f32[128,1024]{1,0:T(8,128)S(1)} collective-permute-done((f32[128,1024]{1,0:T(8,128)}, f32[128,1024]{1,0:T(8,128)S(1)}, u32[]{:S(2)}, u32[]{:S(2)}) %collective-permute-start.5) | collective-permute-done | bytes 524320 | tf_op jit(solution)/shard_map/ppermute | solution.py:357
  130.9 1.4 collective-permute-done.6
  132.3 1.0 all-to-all-done.2.tile_ref.tiles_a.tile_hbm
  133.4 0.0 collective-permute-start.7
  133.4 1.4 collective-permute-start.11
  134.8 0.0 copy-done
  134.8 3.3 %make_send.1 = f32[32,16,128]{2,1,0:T(8,128)} custom-call(f32[32,7,8,128]{3,2,1,0:T(8,128)} %copy-done, f32[576,1024]{1,0:T(8,128)} %get-tuple-element.74.weight_ref, f32[192,128]{1,0:T(8,128)} %get-tuple-element.75.ends_ref, f32[16,1024]{1,0:T(8,128)} %get-tuple-element.76.edge_ref, f32[192,128]{1,0:T(8,128)} %get-tuple-element.77.small_in_ref), custom_call_target="tpu_custom_call" | custom-call | flops 2000000 | bytes 4000000 | tf_op jit(solution)/shard_map/make_send/pallas_call | solution.py:536
  138.1 0.0 collective-permute-done.7.tiles_b
  138.1 0.9 copy-done.7
  139.0 4.4 %block_first_products.1 = (f32[128,1024]{1,0:T(8,128)}, f32[128,1024]{1,0:T(8,128)}, f32[128,1024]{1,0:T(8,128)}, f32[128,1024]{1,0:T(8,128)}) custom-call(s32[1]{0:T(128)} %bitcast.2.place_ref, f32[32,7,8,128]{3,2,1,0:T(8,128)} %copy-done, f32[32,7,8,128]{3,2,1,0:T(8,128)} %copy-done.7, f32[192,1024]{1,0:T(8,128)} %get-tuple-element.59.right_a, ...), custom_call_target="tpu_custom_call" | custom-call | flops 1200000000 | bytes 5000000 | tf_op jit(solution)/shard_map/block_first_products/pallas_call | solution.py:218
  143.5 2.2 %collective-permute-start.9 = (f32[128,1024]{1,0:T(8,128)}, f32[128,1024]{1,0:T(8,128)S(1)}, u32[]{:S(2)}, u32[]{:S(2)}) collective-permute-start(f32[128,1024]{1,0:T(8,128)} %get-tuple-element.82), channel_id=1, source_target_pairs={{0,2},{1,3},{2,4},{3,5},{4,6},{5,7},{6,0},{7,1},{8,10},{9,11},{10,... | collective-permute-start | bytes 1572872 | tf_op jit(solution)/shard_map/ppermute | solution.py:357
  145.7 0.3 collective-permute-start.8
  146.0 1.1 collective-permute-start.10
  147.1 9.0 %all-to-all-start.3 = ((f32[32,16,128]{2,1,0:T(8,128)}), f32[32,16,128]{2,1,0:T(8,128)S(1)}, u32[]{:S(2)}, u32[]{:S(2)}) async-start(f32[32,16,128]{2,1,0:T(8,128)} %make_send.1), calls=%async_computation.3 | async-start | bytes 524288 | tf_op jit(solution)/shard_map/all_to_all | solution.py:677
  156.1 0.0 copy-start.3
  156.2 8.4 %make_inside.1 = (f32[192,1024]{1,0:T(8,128)}, f32[5,1,192]{2,1,0:T(1,128)}, f32[5,1,192]{2,1,0:T(1,128)}) custom-call(f32[192,128]{1,0:T(8,128)} %get-tuple-element.54.halo_ref, f32[192,128]{1,0:T(8,128)} %get-tuple-element.53.column_ref, f32[32,7,8,128]{3,2,1,0:T(8,128)} %copy-done, f32[1,1024,1024]{2,1,0:T(8,128)} %block_hbm.3, f32[192,1024]{1,0:T(8,128)} %bitcast.13, ...), custom_call_target="tpu_custom_call" | custom-call | flops 1200000000 | bytes 8000000 | tf_op jit(solution)/shard_map/make_inside/pallas_call | solution.py:596
  164.6 0.0 copy-start.4
  164.6 0.0 collective-permute-done.11
  164.6 0.0 copy-done.3
  164.6 2.0 %add_bitcast_fusion = f32[1,128,1024]{2,1,0:T(8,128)} fusion(f32[128,1024]{1,0:T(8,128)S(1)} %collective-permute-done.6, f32[128,1024]{1,0:T(8,128)S(1)} %collective-permute-done.5, f32[128,1024]{1,0:T(8,128)S(1)} %copy-done.3, f32[128,1024]{1,0:T(8,128)} %collective-permute-done.11), kind=kLoop, calls=%fused_computation | loop fusion | flops 393216 | bytes 2621440 | tf_op jit(solution)/shard_map/broadcast_in_dim | solution.py:729
  166.7 1.7 all-to-all-done.3.got_ref
  168.3 0.7 copy-done.2
  169.0 2.5 %make_edges.1 = (f32[192,1024]{1,0:T(8,128)}, f32[3,192]{1,0:T(4,128)}, f32[3,192]{1,0:T(4,128)}) custom-call(s32[1]{0:T(128)} %bitcast.4.block_ref, f32[32,16,128]{2,1,0:T(8,128)} %copy-done.2, f32[192,128]{1,0:T(8,128)} %get-tuple-element.53.column_ref, f32[192,1024]{1,0:T(8,128)} %get-tuple-element.87.in_ref), custom_call_target="tpu_custom_call", output_to_operand_aliasing={{0}: (3, {})} | custom-call | flops 200000 | bytes 900000 | tf_op jit(solution)/shard_map/make_edges/pallas_call | solution.py:652
  171.5 0.0 collective-permute-done.9
  171.5 0.0 collective-permute-done.8
  171.5 0.7 collective-permute-done.10
  172.2 0.0 copy-done.4
  172.2 0.9 add_bitcast_fusion.1
  (4 shorter events, 0.0 us)
Async XLA Ops:
  1.7 4.9 %collective-permute-start = (f32[1,192]{1,0:T(1,128)S(1)}, f32[1,192]{1,0:T(1,128)S(1)}, u32[]{:S(2)}, u32[]{:S(2)}) collective-permute-start(f32[1,192]{1,0:T(1,128)S(1)} %copy.19), channel_id=1, source_target_pairs={{0,8},{8,16},{16,24},{24,32},{32,40},{40,48},{48,56},{56,64},{64,7... | collective-permute-start | bytes 2312 | tf_op jit(solution)/shard_map/ppermute | solution.py:141
  5.3 5.5 %collective-permute-start.1 = (f32[1,192]{1,0:T(1,128)S(1)}, f32[1,192]{1,0:T(1,128)S(1)}, u32[]{:S(2)}, u32[]{:S(2)}) collective-permute-start(f32[1,192]{1,0:T(1,128)S(1)} %copy.20), channel_id=1, source_target_pairs={{8,0},{16,8},{24,16},{32,24},{40,32},{48,40},{56,48},{64,56},{72,6... | collective-permute-start | bytes 2312 | tf_op jit(solution)/shard_map/ppermute | solution.py:142
  6.6 4.2 %copy-start.5 = (f32[1,192]{1,0:T(1,128)}, f32[1,192]{1,0:T(1,128)S(1)}, u32[]{:S(2)}) copy-start(f32[1,192]{1,0:T(1,128)S(1)} %collective-permute-done.before_ref) | copy-start | bytes 2308
  10.8 0.6 copy-start.6
  75.5 7.0 %copy-start.8 = (f32[192,1024]{1,0:T(8,128)S(1)}, f32[192,1024]{1,0:T(8,128)}, u32[]{:S(2)}) copy-start(f32[192,1024]{1,0:T(8,128)} %get-tuple-element.59.right_a) | copy-start | bytes 2359300
  77.7 26.5 %all-to-all-start.1 = ((f32[32,6,8,128]{3,2,1,0:T(8,128)}), f32[32,6,8,128]{3,2,1,0:T(8,128)S(1)}, u32[]{:S(2)}, u32[]{:S(2)}) async-start(f32[32,6,8,128]{3,2,1,0:T(8,128)} %butterfly_forward.1), calls=%async_computation.1 | async-start | bytes 1572864 | tf_op jit(solution)/shard_map/all_to_all | solution.py:677
  82.5 12.5 %collective-permute-start.2 = (f32[192,1024]{1,0:T(8,128)S(1)}, f32[192,1024]{1,0:T(8,128)S(1)}, u32[]{:S(2)}, u32[]{:S(2)}) collective-permute-start(f32[192,1024]{1,0:T(8,128)S(1)} %copy-done.8), channel_id=1, source_target_pairs={{0,1},{1,0},{2,3},{3,2},{4,5},{5,4},{6,7},{7,6},{8,9},{9,8},{10,11... | collective-permute-start | bytes 2359304 | tf_op jit(solution)/shard_map/ppermute | solution.py:352
  82.6 13.3 %collective-permute-start.3 = (f32[192,1024]{1,0:T(8,128)}, f32[192,1024]{1,0:T(8,128)}, u32[]{:S(2)}, u32[]{:S(2)}) collective-permute-start(f32[192,1024]{1,0:T(8,128)} %get-tuple-element.60.left_a), channel_id=1, source_target_pairs={{0,1},{1,0},{2,3},{3,2},{4,5},{5,4},{6,7},{7,6},{8,9},{9,8},{10,11... | collective-permute-start | bytes 2359304 | tf_op jit(solution)/shard_map/ppermute | solution.py:352
  95.0 0.9 copy-start.9
  104.2 7.1 %copy-start.1 = (f32[32,6,8,128]{3,2,1,0:T(8,128)}, f32[32,6,8,128]{3,2,1,0:T(8,128)S(1)}, u32[]{:S(2)}) copy-start(f32[32,6,8,128]{3,2,1,0:T(8,128)S(1)} %all-to-all-done.1.right_a.tile_hbm) | copy-start | bytes 2359300
  104.2 29.2 %all-to-all-start.2 = ((f32[32,7,8,128]{3,2,1,0:T(8,128)}), f32[32,7,8,128]{3,2,1,0:T(8,128)S(1)}, u32[]{:S(2)}, u32[]{:S(2)}) async-start(f32[32,7,8,128]{3,2,1,0:T(8,128)} %butterfly_backward.1), calls=%async_computation.2 | async-start | bytes 1835008 | tf_op jit(solution)/shard_map/all_to_all | solution.py:677
  109.0 2.4 %collective-permute-start.4 = (f32[32,6,8,128]{3,2,1,0:T(8,128)S(1)}, f32[32,6,8,128]{3,2,1,0:T(8,128)S(1)}, u32[]{:S(2)}, u32[]{:S(2)}) collective-permute-start(f32[32,6,8,128]{3,2,1,0:T(8,128)S(1)} %all-to-all-done.1.right_a.tile_hbm), channel_id=1, source_target_pairs={{0,1},{1,0},{2,3},{3,2},{4,5},{5,4},{6,7},{7,6},{8,9},{9,8},{10,11... | collective-permute-start | bytes 2359304 | tf_op jit(solution)/shard_map/ppermute | solution.py:352
  111.4 0.9 copy-start.10
  116.7 14.2 %collective-permute-start.5 = (f32[128,1024]{1,0:T(8,128)}, f32[128,1024]{1,0:T(8,128)S(1)}, u32[]{:S(2)}, u32[]{:S(2)}) collective-permute-start(f32[128,1024]{1,0:T(8,128)} %get-tuple-element.71), channel_id=1, source_target_pairs={{0,2},{1,3},{2,4},{3,5},{4,6},{5,7},{6,0},{7,1},{8,10},{9,11},{10,... | collective-permute-start | bytes 1572872 | tf_op jit(solution)/shard_map/ppermute | solution.py:357
  117.2 15.1 %collective-permute-start.6 = (f32[128,1024]{1,0:T(8,128)}, f32[128,1024]{1,0:T(8,128)S(1)}, u32[]{:S(2)}, u32[]{:S(2)}) collective-permute-start(f32[128,1024]{1,0:T(8,128)} %get-tuple-element.72), channel_id=1, source_target_pairs={{0,6},{1,7},{2,0},{3,1},{4,2},{5,3},{6,4},{7,5},{8,14},{9,15},{10,... | collective-permute-start | bytes 1572872 | tf_op jit(solution)/shard_map/ppermute | solution.py:357
  133.4 1.4 copy-start
  133.4 4.7 %collective-permute-start.7 = (f32[32,7,8,128]{3,2,1,0:T(8,128)S(1)}, f32[32,7,8,128]{3,2,1,0:T(8,128)S(1)}, u32[]{:S(2)}, u32[]{:S(2)}) collective-permute-start(f32[32,7,8,128]{3,2,1,0:T(8,128)S(1)} %all-to-all-done.2.tile_ref.tiles_a.tile_hbm), channel_id=1, source_target_pairs={{0,1},{1,0},{2,3},{3,2},{4,5},{5,4},{6,7},{7,6},{8,9},{9,8},{10,11... | collective-permute-start | bytes 2752520 | tf_op jit(solution)/shard_map/ppermute | solution.py:352
  133.4 31.2 %collective-permute-start.11 = (f32[128,1024]{1,0:T(8,128)}, f32[128,1024]{1,0:T(8,128)}, u32[]{:S(2)}, u32[]{:S(2)}) collective-permute-start(f32[128,1024]{1,0:T(8,128)} %get-tuple-element.93), channel_id=1, source_target_pairs={{0,4},{1,5},{2,6},{3,7},{4,0},{5,1},{6,2},{7,3},{8,12},{9,13},{10,... | collective-permute-start | bytes 1572872 | tf_op jit(solution)/shard_map/ppermute | solution.py:357
  138.1 0.9 copy-start.7
  143.5 28.1 %collective-permute-start.9 = (f32[128,1024]{1,0:T(8,128)}, f32[128,1024]{1,0:T(8,128)S(1)}, u32[]{:S(2)}, u32[]{:S(2)}) collective-permute-start(f32[128,1024]{1,0:T(8,128)} %get-tuple-element.82), channel_id=1, source_target_pairs={{0,2},{1,3},{2,4},{3,5},{4,6},{5,7},{6,0},{7,1},{8,10},{9,11},{10,... | collective-permute-start | bytes 1572872 | tf_op jit(solution)/shard_map/ppermute | solution.py:357
  145.7 25.9 %collective-permute-start.8 = (f32[128,1024]{1,0:T(8,128)}, f32[128,1024]{1,0:T(8,128)S(1)}, u32[]{:S(2)}, u32[]{:S(2)}) collective-permute-start(f32[128,1024]{1,0:T(8,128)} %get-tuple-element.83), channel_id=1, source_target_pairs={{0,4},{1,5},{2,6},{3,7},{4,0},{5,1},{6,2},{7,3},{8,12},{9,13},{10,... | collective-permute-start | bytes 1572872 | tf_op jit(solution)/shard_map/ppermute | solution.py:357
  146.0 26.2 %collective-permute-start.10 = (f32[128,1024]{1,0:T(8,128)}, f32[128,1024]{1,0:T(8,128)S(1)}, u32[]{:S(2)}, u32[]{:S(2)}) collective-permute-start(f32[128,1024]{1,0:T(8,128)} %get-tuple-element.84), channel_id=1, source_target_pairs={{0,6},{1,7},{2,0},{3,1},{4,2},{5,3},{6,4},{7,5},{8,14},{9,15},{10,... | collective-permute-start | bytes 1572872 | tf_op jit(solution)/shard_map/ppermute | solution.py:357
  147.1 21.2 %all-to-all-start.3 = ((f32[32,16,128]{2,1,0:T(8,128)}), f32[32,16,128]{2,1,0:T(8,128)S(1)}, u32[]{:S(2)}, u32[]{:S(2)}) async-start(f32[32,16,128]{2,1,0:T(8,128)} %make_send.1), calls=%async_computation.3 | async-start | bytes 524288 | tf_op jit(solution)/shard_map/all_to_all | solution.py:677
  156.1 8.5 %copy-start.3 = (f32[128,1024]{1,0:T(8,128)S(1)}, f32[128,1024]{1,0:T(8,128)}, u32[]{:S(2)}) copy-start(f32[128,1024]{1,0:T(8,128)} %get-tuple-element.92) | copy-start | bytes 1572868
  164.6 7.6 %copy-start.4 = (f32[128,1024]{1,0:T(8,128)S(1)}, f32[128,1024]{1,0:T(8,128)}, u32[]{:S(2)}) copy-start(f32[128,1024]{1,0:T(8,128)} %get-tuple-element.91) | copy-start | bytes 1572868
  168.3 0.7 copy-start.2

commit v2 on v1

--- a/solution.py
+++ b/solution.py
@@ -190,7 +190,8 @@
 
 
 def first_kernel(place_ref, tiles_a, tiles_b, right_a, right_b, *refs):
-    outs, (left_ref, tile_ref, right_ref, sem) = refs[:CHIPS], refs[CHIPS:]
+    outs, (left_ref, tile_ref, right_ref, total_ref, sem) = refs[:CHIPS], refs[CHIPS:]
+    puts = []
     copies = []
     for half, (tiles, right) in enumerate(((tiles_a, right_a), (tiles_b, right_b))):
         copies.append(pltpu.make_async_copy(right, right_ref.at[half], sem.at[2 * half]))
@@ -208,9 +209,13 @@
                 left_ref[step, 8 * group : 8 * group + 8, :] = tile_ref[half, owner, tile]
             product = dot_three(split_two(left_ref[step] * WIDTH_SCALE), right, 0, 0)
             if half == 0:
-                outs[step][...] = product
+                total_ref[step] = product
             else:
-                outs[step][...] += product
+                total_ref[step] += product
+                puts.append(pltpu.make_async_copy(total_ref.at[step], outs[step], sem.at[4 + step]))
+                puts[-1].start()
+    for put in puts:
+        put.wait()
 
 
 def first_products(place, tiles, tiles_other, gated, gated_other):
@@ -219,12 +224,13 @@
         first_kernel,
         out_shape=[piece] * CHIPS,
         in_specs=[pl.BlockSpec(memory_space=pltpu.SMEM)] + [IN_HBM] * 4,
-        out_specs=[pl.BlockSpec()] * CHIPS,
+        out_specs=[IN_HBM] * CHIPS,
         scratch_shapes=[
             pltpu.VMEM((CHIPS, 192, 128), jnp.float32),
             pltpu.VMEM((2,) + tiles.shape, jnp.float32),
             pltpu.VMEM((2,) + gated.shape, jnp.float32),
-            pltpu.SemaphoreType.DMA((4,)),
+            pltpu.VMEM((CHIPS, 128, 1024), jnp.float32),
+            pltpu.SemaphoreType.DMA((8,)),
         ],
         compiler_params=pltpu.CompilerParams(vmem_limit_bytes=VMEM_LIMIT),
         cost_estimate=pl.CostEstimate(flops=1_200_000_000, bytes_accessed=5_000_000, transcendentals=0),

time: 174 us -> 174 us (level)
  no operation moved by 1% of the time
where the time goes in v2:
time: 174 us; the launch traced here: 173 us
  Pallas kernels  56.2 us (32%)
  blocking collectives  54.8 us (31%)
  starting transfers between devices  31.1 us (18%)
  waiting for transfers between devices  22.2 us (13%)
  local copies, waits for them, and re-layouts  5.15 us (3%)
  other arithmetic  2.97 us (2%)
    all_to_all x1, blocking collectives, local(): swap = lambda tiles: lax.all_to_all(tiles, 'seq', 0, 0, tiled=True)  54.8 us
    all_to_all x3, starting transfers between devices, local(): swap = lambda tiles: lax.all_to_all(tiles, 'seq', 0, 0, tiled=True)  18.5 us
    all_to_all x3, waiting for transfers between devices, local(): swap = lambda tiles: lax.all_to_all(tiles, 'seq', 0, 0, tiled=True)  11 us
    pallas_call x1, Pallas kernels, make_output(): pl.pallas_call(output_kernel, out_shape=[full, full, jax.ShapeDtypeStruct...  9.5 us
    pallas_call x1, Pallas kernels, prologue(): pl.pallas_call(prologue_kernel, grid=(height // COLUMNS,), out_shape=[jax...  9.34 us
    pallas_call x1, Pallas kernels, make_inside(): pl.pallas_call(inside_kernel, out_shape=[jax.ShapeDtypeStruct(signal.shap...  8.43 us
    pallas_call x1, Pallas kernels, tap_weights(): pl.pallas_call(tap_kernel, grid=(height // COLUMNS,), out_shape=[jax.Shap...  7.92 us
    ppermute x6, starting transfers between devices, receive_pieces(): lax.ppermute(pieces[step], 'ch', [(i, (i + 2 * step) % (2 * CHIPS)) for i...  7.05 us
  transfers between devices with their start and end apart: 15, of which 8 were waited for; matrix products, arithmetic and copies ran while one was open for 1% of the time, Pallas kernels for 26%

profile of v2, /device:TPU:6, one launch (start us, length us, event | category | flops | bytes accessed | tf_op | source)
XLA Modules:
  0.0 173.2 jit_solution(5136020506520807481)
XLA Ops:
  0.6 1.0 fusion
  1.7 0.1 copy.19
  1.7 3.5 %collective-permute-start = (f32[1,192]{1,0:T(1,128)S(1)}, f32[1,192]{1,0:T(1,128)S(1)}, u32[]{:S(2)}, u32[]{:S(2)}) collective-permute-start(f32[1,192]{1,0:T(1,128)S(1)} %copy.19), channel_id=1, source_target_pairs={{0,8},{8,16},{16,24},{24,32},{32,40},{40,48},{48,56},{56,64},{64,7... | collective-permute-start | bytes 2312 | tf_op jit(solution)/shard_map/ppermute | solution.py:141
  5.2 0.1 copy.20
  5.3 1.3 collective-permute-start.1
  6.6 0.0 collective-permute-done.before_ref
  6.6 0.0 copy-start.5
  6.6 4.1 %collective-permute-done.1.after_ref = f32[1,192]{1,0:T(1,128)S(1)} collective-permute-done((f32[1,192]{1,0:T(1,128)S(1)}, f32[1,192]{1,0:T(1,128)S(1)}, u32[]{:S(2)}, u32[]{:S(2)}) %collective-permute-start.1) | collective-permute-done | bytes 800 | tf_op jit(solution)/shard_map/ppermute | solution.py:142
  10.8 0.0 copy-start.6
  10.8 0.0 copy-done.5
  10.8 0.6 copy-done.6
  11.3 9.3 %prologue.1 = (f32[32,13,8,128]{3,2,1,0:T(8,128)}, f32[192,1024]{1,0:T(8,128)}, f32[192,1024]{1,0:T(8,128)}, f32[192,128]{1,0:T(8,128)}, f32[192,128]{1,0:T(8,128)}) custom-call(f32[192,1024]{1,0:T(8,128)} %bitcast.10, f32[192,1024]{1,0:T(8,128)} %bitcast.14, f32[1,192]{1,0:T(1,128)} %copy-done.5, f32[1,192]{1,0:T(1,128)} %copy-done.6, f32[3,192]{1,0:T(4,128)} %taps_q_ref.1, ...), custom_call_target="tpu_custom_call" | custom-call | flops 2400000000 | bytes 15000000 | tf_op jit(solution)/shard_map/prologue/pallas_call | solution.py:317
  20.7 54.8 %all_to_all.20.in_ref = f32[32,13,8,128]{3,2,1,0:T(8,128)S(1)} all-to-all(f32[32,13,8,128]{3,2,1,0:T(8,128)} %get-tuple-element.55), channel_id=1, replica_groups=mesh['seq'=32,'ch'=8] {'seq'}, dimensions={0} | all-to-all | bytes 3407872 | tf_op jit(solution)/shard_map/all_to_all | solution.py:683
  75.5 0.0 copy-start.8
  75.5 2.3 %butterfly_forward.1 = f32[32,6,8,128]{3,2,1,0:T(8,128)} custom-call(f32[32,13,8,128]{3,2,1,0:T(8,128)S(1)} %all_to_all.20.in_ref), custom_call_target="tpu_custom_call" | custom-call | flops 4000000 | bytes 1800000 | tf_op jit(solution)/shard_map/butterfly_forward/pallas_call | solution.py:110
  77.7 4.7 %all-to-all-start.1 = ((f32[32,6,8,128]{3,2,1,0:T(8,128)}), f32[32,6,8,128]{3,2,1,0:T(8,128)S(1)}, u32[]{:S(2)}, u32[]{:S(2)}) async-start(f32[32,6,8,128]{3,2,1,0:T(8,128)} %butterfly_forward.1), calls=%async_computation.1 | async-start | bytes 1572864 | tf_op jit(solution)/shard_map/all_to_all | solution.py:683
  82.5 0.0 copy-done.8
  82.5 0.1 collective-permute-start.2
  82.6 0.5 collective-permute-start.3
  83.1 7.9 %tap_weights.1 = (f32[576,1024]{1,0:T(8,128)}, f32[192,128]{1,0:T(8,128)}, f32[16,1024]{1,0:T(8,128)}) custom-call(f32[192,128]{1,0:T(8,128)} %get-tuple-element.54.halo_ref, f32[192,1024]{1,0:T(8,128)} %bitcast.11, f32[1,1024,1024]{2,1,0:T(8,128)} %block_hbm.3), custom_call_target="tpu_custom_call" | custom-call | flops 3600000000 | bytes 8000000 | tf_op jit(solution)/shard_map/tap_weights/pallas_call | solution.py:485
  91.0 4.0 %butterfly_backward.1 = f32[32,7,8,128]{3,2,1,0:T(8,128)} custom-call(f32[32,13,8,128]{3,2,1,0:T(8,128)S(1)} %all_to_all.20.in_ref), custom_call_target="tpu_custom_call" | custom-call | flops 12000000 | bytes 2600000 | tf_op jit(solution)/shard_map/butterfly_backward/pallas_call | solution.py:123
  95.0 0.0 collective-permute-done.2.right_b
  95.0 0.0 copy-start.9
  95.0 0.9 copy-done.9
  95.9 0.0 collective-permute-done.3.left_b
  95.9 8.4 %all-to-all-done.1.right_a.tile_hbm = f32[32,6,8,128]{3,2,1,0:T(8,128)S(1)} async-done(((f32[32,6,8,128]{3,2,1,0:T(8,128)}), f32[32,6,8,128]{3,2,1,0:T(8,128)S(1)}, u32[]{:S(2)}, u32[]{:S(2)}) %all-to-all-start.1) | async-done | bytes 786464 | tf_op jit(solution)/shard_map/all_to_all | solution.py:683
  104.2 0.0 copy-start.1
  104.2 4.8 %all-to-all-start.2 = ((f32[32,7,8,128]{3,2,1,0:T(8,128)}), f32[32,7,8,128]{3,2,1,0:T(8,128)S(1)}, u32[]{:S(2)}, u32[]{:S(2)}) async-start(f32[32,7,8,128]{3,2,1,0:T(8,128)} %butterfly_backward.1), calls=%async_computation.2 | async-start | bytes 1835008 | tf_op jit(solution)/shard_map/all_to_all | solution.py:683
  109.0 0.1 collective-permute-start.4
  109.1 2.3 %collective-permute-done.4.right_b = f32[32,6,8,128]{3,2,1,0:T(8,128)S(1)} collective-permute-done((f32[32,6,8,128]{3,2,1,0:T(8,128)S(1)}, f32[32,6,8,128]{3,2,1,0:T(8,128)S(1)}, u32[]{:S(2)}, u32[]{:S(2)}) %collective-permute-start.4) | collective-permute-done | bytes 786464 | tf_op jit(solution)/shard_map/ppermute | solution.py:358
  111.4 0.0 copy-done.1
  111.4 0.9 copy-done.10
  112.2 4.5 %block_second_products.1 = (f32[128,1024]{1,0:T(8,128)}, f32[128,1024]{1,0:T(8,128)}, f32[128,1024]{1,0:T(8,128)}, f32[128,1024]{1,0:T(8,128)}) custom-call(s32[1]{0:T(128)} %bitcast.2.place_ref, f32[192,1024]{1,0:T(8,128)} %get-tuple-element.60.left_a, f32[192,1024]{1,0:T(8,128)} %collective-permute-done.3.left_b, f32[32,6,8,128]{3,2,1,0:T(8,128)} %copy-done.1, ...), custom_call_target="tpu_custom_call" | custom-call | flops 1200000000 | bytes 5000000 | tf_op jit(solution)/shard_map/block_second_products/pallas_call | solution.py:345
  116.7 0.5 collective-permute-start.5
  117.2 1.5 collective-permute-start.6
  118.8 9.5 %make_output.1 = (f32[192,1024]{1,0:T(8,128)}, f32[192,1024]{1,0:T(8,128)}, f32[192,128]{1,0:T(8,128)}) custom-call(f32[192,128]{1,0:T(8,128)} %get-tuple-element.53.column_ref, f32[192,128]{1,0:T(8,128)} %get-tuple-element.54.halo_ref, f32[32,6,8,128]{3,2,1,0:T(8,128)} %copy-done.1, f32[1,1024,1024]{2,1,0:T(8,128)} %block_hbm.2, f32[192,1024]{1,0:T(8,128)} %bitcast.12, ...), custom_call_target="tpu_custom_call" | custom-call | flops 1200000000 | bytes 9000000 | tf_op jit(solution)/shard_map/make_output/pallas_call | solution.py:439
  128.3 2.7 %collective-permute-done.5 = f32[128,1024]{1,0:T(8,128)S(1)} collective-permute-done((f32[128,1024]{1,0:T(8,128)}, f32[128,1024]{1,0:T(8,128)S(1)}, u32[]{:S(2)}, u32[]{:S(2)}) %collective-permute-start.5) | collective-permute-done | bytes 524320 | tf_op jit(solution)/shard_map/ppermute | solution.py:363
  130.9 1.4 collective-permute-done.6
  132.3 1.0 all-to-all-done.2.tile_ref.tiles_a.tile_hbm
  133.4 0.0 collective-permute-start.7
  133.4 1.4 collective-permute-start.11
  134.8 0.0 copy-done
  134.8 3.3 %make_send.1 = f32[32,16,128]{2,1,0:T(8,128)} custom-call(f32[32,7,8,128]{3,2,1,0:T(8,128)} %copy-done, f32[576,1024]{1,0:T(8,128)} %get-tuple-element.74.weight_ref, f32[192,128]{1,0:T(8,128)} %get-tuple-element.75.ends_ref, f32[16,1024]{1,0:T(8,128)} %get-tuple-element.76.edge_ref, f32[192,128]{1,0:T(8,128)} %get-tuple-element.77.small_in_ref), custom_call_target="tpu_custom_call" | custom-call | flops 2000000 | bytes 4000000 | tf_op jit(solution)/shard_map/make_send/pallas_call | solution.py:542
  138.1 0.0 collective-permute-done.7.tiles_b
  138.1 0.9 copy-done.7
  139.0 4.5 %block_first_products.1 = (f32[128,1024]{1,0:T(8,128)}, f32[128,1024]{1,0:T(8,128)}, f32[128,1024]{1,0:T(8,128)}, f32[128,1024]{1,0:T(8,128)}) custom-call(s32[1]{0:T(128)} %bitcast.2.place_ref, f32[32,7,8,128]{3,2,1,0:T(8,128)} %copy-done, f32[32,7,8,128]{3,2,1,0:T(8,128)} %copy-done.7, f32[192,1024]{1,0:T(8,128)} %get-tuple-element.59.right_a, ...), custom_call_target="tpu_custom_call" | custom-call | flops 1200000000 | bytes 5000000 | tf_op jit(solution)/shard_map/block_first_products/pallas_call | solution.py:223
  143.5 2.2 %collective-permute-start.9 = (f32[128,1024]{1,0:T(8,128)}, f32[128,1024]{1,0:T(8,128)S(1)}, u32[]{:S(2)}, u32[]{:S(2)}) collective-permute-start(f32[128,1024]{1,0:T(8,128)} %get-tuple-element.82), channel_id=1, source_target_pairs={{0,2},{1,3},{2,4},{3,5},{4,6},{5,7},{6,0},{7,1},{8,10},{9,11},{10,... | collective-permute-start | bytes 1572872 | tf_op jit(solution)/shard_map/ppermute | solution.py:363
  145.7 0.3 collective-permute-start.8
  146.0 1.1 collective-permute-start.10
  147.2 9.1 %all-to-all-start.3 = ((f32[32,16,128]{2,1,0:T(8,128)}), f32[32,16,128]{2,1,0:T(8,128)S(1)}, u32[]{:S(2)}, u32[]{:S(2)}) async-start(f32[32,16,128]{2,1,0:T(8,128)} %make_send.1), calls=%async_computation.3 | async-start | bytes 524288 | tf_op jit(solution)/shard_map/all_to_all | solution.py:683
  156.2 0.0 copy-start.3
  156.2 8.4 %make_inside.1 = (f32[192,1024]{1,0:T(8,128)}, f32[5,1,192]{2,1,0:T(1,128)}, f32[5,1,192]{2,1,0:T(1,128)}) custom-call(f32[192,128]{1,0:T(8,128)} %get-tuple-element.54.halo_ref, f32[192,128]{1,0:T(8,128)} %get-tuple-element.53.column_ref, f32[32,7,8,128]{3,2,1,0:T(8,128)} %copy-done, f32[1,1024,1024]{2,1,0:T(8,128)} %block_hbm.3, f32[192,1024]{1,0:T(8,128)} %bitcast.13, ...), custom_call_target="tpu_custom_call" | custom-call | flops 1200000000 | bytes 8000000 | tf_op jit(solution)/shard_map/make_inside/pallas_call | solution.py:602
  164.7 0.0 copy-start.4
  164.7 0.0 collective-permute-done.11
  164.7 0.0 copy-done.3
  164.7 2.0 %add_bitcast_fusion = f32[1,128,1024]{2,1,0:T(8,128)} fusion(f32[128,1024]{1,0:T(8,128)S(1)} %collective-permute-done.6, f32[128,1024]{1,0:T(8,128)S(1)} %collective-permute-done.5, f32[128,1024]{1,0:T(8,128)S(1)} %copy-done.3, f32[128,1024]{1,0:T(8,128)} %collective-permute-done.11), kind=kLoop, calls=%fused_computation | loop fusion | flops 393216 | bytes 2621440 | tf_op jit(solution)/shard_map/broadcast_in_dim | solution.py:735
  166.7 1.6 all-to-all-done.3.got_ref
  168.4 0.7 copy-done.2
  169.1 2.5 %make_edges.1 = (f32[192,1024]{1,0:T(8,128)}, f32[3,192]{1,0:T(4,128)}, f32[3,192]{1,0:T(4,128)}) custom-call(s32[1]{0:T(128)} %bitcast.4.block_ref, f32[32,16,128]{2,1,0:T(8,128)} %copy-done.2, f32[192,128]{1,0:T(8,128)} %get-tuple-element.53.column_ref, f32[192,1024]{1,0:T(8,128)} %get-tuple-element.87.in_ref), custom_call_target="tpu_custom_call", output_to_operand_aliasing={{0}: (3, {})} | custom-call | flops 200000 | bytes 900000 | tf_op jit(solution)/shard_map/make_edges/pallas_call | solution.py:658
  171.5 0.0 collective-permute-done.9
  171.6 0.0 collective-permute-done.8
  171.6 0.7 collective-permute-done.10
  172.2 0.0 copy-done.4
  172.2 0.9 add_bitcast_fusion.1
  (4 shorter events, 0.0 us)
Async XLA Ops:
  1.7 4.9 %collective-permute-start = (f32[1,192]{1,0:T(1,128)S(1)}, f32[1,192]{1,0:T(1,128)S(1)}, u32[]{:S(2)}, u32[]{:S(2)}) collective-permute-start(f32[1,192]{1,0:T(1,128)S(1)} %copy.19), channel_id=1, source_target_pairs={{0,8},{8,16},{16,24},{24,32},{32,40},{40,48},{48,56},{56,64},{64,7... | collective-permute-start | bytes 2312 | tf_op jit(solution)/shard_map/ppermute | solution.py:141
  5.3 5.5 %collective-permute-start.1 = (f32[1,192]{1,0:T(1,128)S(1)}, f32[1,192]{1,0:T(1,128)S(1)}, u32[]{:S(2)}, u32[]{:S(2)}) collective-permute-start(f32[1,192]{1,0:T(1,128)S(1)} %copy.20), channel_id=1, source_target_pairs={{8,0},{16,8},{24,16},{32,24},{40,32},{48,40},{56,48},{64,56},{72,6... | collective-permute-start | bytes 2312 | tf_op jit(solution)/shard_map/ppermute | solution.py:142
  6.6 4.2 %copy-start.5 = (f32[1,192]{1,0:T(1,128)}, f32[1,192]{1,0:T(1,128)S(1)}, u32[]{:S(2)}) copy-start(f32[1,192]{1,0:T(1,128)S(1)} %collective-permute-done.before_ref) | copy-start | bytes 2308
  10.8 0.6 copy-start.6
  75.5 7.0 %copy-start.8 = (f32[192,1024]{1,0:T(8,128)S(1)}, f32[192,1024]{1,0:T(8,128)}, u32[]{:S(2)}) copy-start(f32[192,1024]{1,0:T(8,128)} %get-tuple-element.59.right_a) | copy-start | bytes 2359300
  77.7 26.5 %all-to-all-start.1 = ((f32[32,6,8,128]{3,2,1,0:T(8,128)}), f32[32,6,8,128]{3,2,1,0:T(8,128)S(1)}, u32[]{:S(2)}, u32[]{:S(2)}) async-start(f32[32,6,8,128]{3,2,1,0:T(8,128)} %butterfly_forward.1), calls=%async_computation.1 | async-start | bytes 1572864 | tf_op jit(solution)/shard_map/all_to_all | solution.py:683
  82.5 12.5 %collective-permute-start.2 = (f32[192,1024]{1,0:T(8,128)S(1)}, f32[192,1024]{1,0:T(8,128)S(1)}, u32[]{:S(2)}, u32[]{:S(2)}) collective-permute-start(f32[192,1024]{1,0:T(8,128)S(1)} %copy-done.8), channel_id=1, source_target_pairs={{0,1},{1,0},{2,3},{3,2},{4,5},{5,4},{6,7},{7,6},{8,9},{9,8},{10,11... | collective-permute-start | bytes 2359304 | tf_op jit(solution)/shard_map/ppermute | solution.py:358
  82.6 13.3 %collective-permute-start.3 = (f32[192,1024]{1,0:T(8,128)}, f32[192,1024]{1,0:T(8,128)}, u32[]{:S(2)}, u32[]{:S(2)}) collective-permute-start(f32[192,1024]{1,0:T(8,128)} %get-tuple-element.60.left_a), channel_id=1, source_target_pairs={{0,1},{1,0},{2,3},{3,2},{4,5},{5,4},{6,7},{7,6},{8,9},{9,8},{10,11... | collective-permute-start | bytes 2359304 | tf_op jit(solution)/shard_map/ppermute | solution.py:358
  95.0 0.9 copy-start.9
  104.2 7.1 %copy-start.1 = (f32[32,6,8,128]{3,2,1,0:T(8,128)}, f32[32,6,8,128]{3,2,1,0:T(8,128)S(1)}, u32[]{:S(2)}) copy-start(f32[32,6,8,128]{3,2,1,0:T(8,128)S(1)} %all-to-all-done.1.right_a.tile_hbm) | copy-start | bytes 2359300
  104.2 29.2 %all-to-all-start.2 = ((f32[32,7,8,128]{3,2,1,0:T(8,128)}), f32[32,7,8,128]{3,2,1,0:T(8,128)S(1)}, u32[]{:S(2)}, u32[]{:S(2)}) async-start(f32[32,7,8,128]{3,2,1,0:T(8,128)} %butterfly_backward.1), calls=%async_computation.2 | async-start | bytes 1835008 | tf_op jit(solution)/shard_map/all_to_all | solution.py:683
  109.0 2.4 %collective-permute-start.4 = (f32[32,6,8,128]{3,2,1,0:T(8,128)S(1)}, f32[32,6,8,128]{3,2,1,0:T(8,128)S(1)}, u32[]{:S(2)}, u32[]{:S(2)}) collective-permute-start(f32[32,6,8,128]{3,2,1,0:T(8,128)S(1)} %all-to-all-done.1.right_a.tile_hbm), channel_id=1, source_target_pairs={{0,1},{1,0},{2,3},{3,2},{4,5},{5,4},{6,7},{7,6},{8,9},{9,8},{10,11... | collective-permute-start | bytes 2359304 | tf_op jit(solution)/shard_map/ppermute | solution.py:358
  111.4 0.9 copy-start.10
  116.7 14.2 %collective-permute-start.5 = (f32[128,1024]{1,0:T(8,128)}, f32[128,1024]{1,0:T(8,128)S(1)}, u32[]{:S(2)}, u32[]{:S(2)}) collective-permute-start(f32[128,1024]{1,0:T(8,128)} %get-tuple-element.71), channel_id=1, source_target_pairs={{0,2},{1,3},{2,4},{3,5},{4,6},{5,7},{6,0},{7,1},{8,10},{9,11},{10,... | collective-permute-start | bytes 1572872 | tf_op jit(solution)/shard_map/ppermute | solution.py:363
  117.2 15.1 %collective-permute-start.6 = (f32[128,1024]{1,0:T(8,128)}, f32[128,1024]{1,0:T(8,128)S(1)}, u32[]{:S(2)}, u32[]{:S(2)}) collective-permute-start(f32[128,1024]{1,0:T(8,128)} %get-tuple-element.72), channel_id=1, source_target_pairs={{0,6},{1,7},{2,0},{3,1},{4,2},{5,3},{6,4},{7,5},{8,14},{9,15},{10,... | collective-permute-start | bytes 1572872 | tf_op jit(solution)/shard_map/ppermute | solution.py:363
  133.4 1.4 copy-start
  133.4 4.7 %collective-permute-start.7 = (f32[32,7,8,128]{3,2,1,0:T(8,128)S(1)}, f32[32,7,8,128]{3,2,1,0:T(8,128)S(1)}, u32[]{:S(2)}, u32[]{:S(2)}) collective-permute-start(f32[32,7,8,128]{3,2,1,0:T(8,128)S(1)} %all-to-all-done.2.tile_ref.tiles_a.tile_hbm), channel_id=1, source_target_pairs={{0,1},{1,0},{2,3},{3,2},{4,5},{5,4},{6,7},{7,6},{8,9},{9,8},{10,11... | collective-permute-start | bytes 2752520 | tf_op jit(solution)/shard_map/ppermute | solution.py:358
  133.4 31.3 %collective-permute-start.11 = (f32[128,1024]{1,0:T(8,128)}, f32[128,1024]{1,0:T(8,128)}, u32[]{:S(2)}, u32[]{:S(2)}) collective-permute-start(f32[128,1024]{1,0:T(8,128)} %get-tuple-element.93), channel_id=1, source_target_pairs={{0,4},{1,5},{2,6},{3,7},{4,0},{5,1},{6,2},{7,3},{8,12},{9,13},{10,... | collective-permute-start | bytes 1572872 | tf_op jit(solution)/shard_map/ppermute | solution.py:363
  138.1 0.9 copy-start.7
  143.5 28.0 %collective-permute-start.9 = (f32[128,1024]{1,0:T(8,128)}, f32[128,1024]{1,0:T(8,128)S(1)}, u32[]{:S(2)}, u32[]{:S(2)}) collective-permute-start(f32[128,1024]{1,0:T(8,128)} %get-tuple-element.82), channel_id=1, source_target_pairs={{0,2},{1,3},{2,4},{3,5},{4,6},{5,7},{6,0},{7,1},{8,10},{9,11},{10,... | collective-permute-start | bytes 1572872 | tf_op jit(solution)/shard_map/ppermute | solution.py:363
  145.7 25.9 %collective-permute-start.8 = (f32[128,1024]{1,0:T(8,128)}, f32[128,1024]{1,0:T(8,128)S(1)}, u32[]{:S(2)}, u32[]{:S(2)}) collective-permute-start(f32[128,1024]{1,0:T(8,128)} %get-tuple-element.83), channel_id=1, source_target_pairs={{0,4},{1,5},{2,6},{3,7},{4,0},{5,1},{6,2},{7,3},{8,12},{9,13},{10,... | collective-permute-start | bytes 1572872 | tf_op jit(solution)/shard_map/ppermute | solution.py:363
  146.0 26.2 %collective-permute-start.10 = (f32[128,1024]{1,0:T(8,128)}, f32[128,1024]{1,0:T(8,128)S(1)}, u32[]{:S(2)}, u32[]{:S(2)}) collective-permute-start(f32[128,1024]{1,0:T(8,128)} %get-tuple-element.84), channel_id=1, source_target_pairs={{0,6},{1,7},{2,0},{3,1},{4,2},{5,3},{6,4},{7,5},{8,14},{9,15},{10,... | collective-permute-start | bytes 1572872 | tf_op jit(solution)/shard_map/ppermute | solution.py:363
  147.2 21.2 %all-to-all-start.3 = ((f32[32,16,128]{2,1,0:T(8,128)}), f32[32,16,128]{2,1,0:T(8,128)S(1)}, u32[]{:S(2)}, u32[]{:S(2)}) async-start(f32[32,16,128]{2,1,0:T(8,128)} %make_send.1), calls=%async_computation.3 | async-start | bytes 524288 | tf_op jit(solution)/shard_map/all_to_all | solution.py:683
  156.2 8.5 %copy-start.3 = (f32[128,1024]{1,0:T(8,128)S(1)}, f32[128,1024]{1,0:T(8,128)}, u32[]{:S(2)}) copy-start(f32[128,1024]{1,0:T(8,128)} %get-tuple-element.92) | copy-start | bytes 1572868
  164.7 7.6 %copy-start.4 = (f32[128,1024]{1,0:T(8,128)S(1)}, f32[128,1024]{1,0:T(8,128)}, u32[]{:S(2)}) copy-start(f32[128,1024]{1,0:T(8,128)} %get-tuple-element.91) | copy-start | bytes 1572868
  168.4 0.7 copy-start.2
